TPU v7x, 512 devices: a whole 4x8x8 slice. The times are simulated.
512 devices in a mesh: stream: 32 (over x, y_hi, core), cross: 16 (over z, y_lo).
Axes of the slice: x: 4, y: 8 (y_hi: 4, y_lo: 2; y = y_hi * 2 + y_lo), z: 8, core: 2. Of those that a mesh axis runs over, the one named last changes fastest.
Arguments:
- latents: bfloat16 [262144, 128], P(('stream', 'cross')), may hold values from -6 to 6
- stale_latents: bfloat16 [262144, 128], P(('stream', 'cross')), may hold values from -6 to 6
- edge_latents: bfloat16 [786432, 128], P(('stream', 'cross')), may hold values from -6 to 6
- senders: int32 [786432], P(('stream', 'cross')), may hold values from 0 to 1023
- receivers: int32 [786432], P(('stream', 'cross')), may hold values from 0 to 511
- edge_count: int32 [512], P(('stream', 'cross')), may hold values from 512 to 1536, as said below
- send_list: int32 [512, 4, 128], P(('stream', 'cross')), may hold values from 0 to 511
- node_cotangent: bfloat16 [262144, 128], P(('stream', 'cross')), may hold values from -6 to 6
- edge_cotangent: bfloat16 [786432, 128], P(('stream', 'cross')), may hold values from -6 to 6
- edge_first: bfloat16 [384, 128], replicated, may hold values from -0.3125 to 0.3125
- edge_bias: float32 [128], replicated, may hold values from -3 to 3
- edge_second: bfloat16 [128, 128], replicated, may hold values from -0.5 to 0.5
- edge_gain: float32 [128], replicated, may hold values from 0.25 to 1.75
- node_first: bfloat16 [256, 128], replicated, may hold values from -0.375 to 0.375
- node_bias: float32 [128], replicated, may hold values from -3 to 3
- node_second: bfloat16 [128, 128], replicated, may hold values from -0.5 to 0.5
- node_gain: float32 [128], replicated, may hold values from 0.25 to 1.75
Outputs:
- new_latents: bfloat16 [262144, 128], P(('stream', 'cross'))
- latent_grads: bfloat16 [262144, 128], P(('stream', 'cross'))
- stale_grads: bfloat16 [262144, 128], P(('stream', 'cross'))
- edge_grads: bfloat16 [786432, 128], P(('stream', 'cross'))
- edge_first_grad: float32 [384, 128], replicated
- edge_bias_grad: float32 [128], replicated
- edge_second_grad: float32 [128, 128], replicated
- edge_gain_grad: float32 [128], replicated
- node_first_grad: float32 [256, 128], replicated
- node_bias_grad: float32 [128], replicated
- node_second_grad: float32 [128, 128], replicated
- node_gain_grad: float32 [128], replicated
Inputs may be any that keep to these rules, and one draw needn't show every extreme that they name: `edge_count`: a partition's live edge slots come first; some partition has 1536 live slots. `senders`: rows below 512 are the partition's own nodes, the rest its four halo blocks in the order of the steps. `send_list`: a row may be listed more than once.
All inputs are finite; a program needn't handle non-finite values.
Results may differ from a plain program's by a relative error of at most 0.015.
Values may be sent and summed in bfloat16 or wider, within the bound.
A program may use at most 64 MiB of HBM per device.

v0:
```python
import math

import jax
import jax.numpy as jnp
from jax import lax
from jax.sharding import PartitionSpec as P

EPSILON = 1e-05


def extended(shard, sides, width):
    for axis, dim in sides:
        size, length = (lax.axis_size(axis), shard.shape[dim])
        up = [(i, (i + 1) % size) for i in range(size - 1)]
        down = [(j, i) for i, j in up]
        last = lax.slice_in_dim(shard, length - width, length, axis=dim)
        initial = lax.slice_in_dim(shard, 0, width, axis=dim)
        before = lax.ppermute(last, axis, up)
        after = lax.ppermute(initial, axis, down)
        shard = jnp.concatenate([before, shard, after], axis=dim)
    return shard


def layer_norm(values, scale_gain):
    row_mean = jnp.mean(values, axis=-1, keepdims=True)
    centered = values - row_mean
    variance = jnp.mean(centered * centered, axis=-1, keepdims=True)
    return centered * lax.rsqrt(variance + EPSILON) * scale_gain


def local_layer(owned, halo_rows, edge_rows, params, senders, receivers, edge_total):
    edge_first, edge_bias, edge_second, edge_gain, node_first, node_bias, node_second, node_gain = (
        params
    )
    node_table = jnp.concatenate([owned, halo_rows], axis=0)
    sender_rows = jnp.take(node_table, senders, axis=0)
    receiver_rows = jnp.take(owned, receivers, axis=0)
    joined = jnp.concatenate([edge_rows, sender_rows, receiver_rows], axis=1).astype(jnp.bfloat16)
    hidden_pre = jnp.dot(joined, edge_first, preferred_element_type=jnp.float32) + edge_bias
    edge_hidden = jax.nn.silu(hidden_pre).astype(jnp.bfloat16)
    edge_out = jnp.dot(edge_hidden, edge_second, preferred_element_type=jnp.float32)
    edge_alive = (jnp.arange(edge_rows.shape[0], dtype=jnp.int32) < edge_total).astype(jnp.float32)[
        :, None
    ]
    new_edges = (edge_rows + edge_alive * layer_norm(edge_out, edge_gain)).astype(jnp.bfloat16)
    summed = (
        jnp.zeros(owned.shape, jnp.float32)
        .at[receivers]
        .add(edge_alive * new_edges.astype(jnp.float32))
    )
    node_input = jnp.concatenate([owned, summed], axis=1).astype(jnp.bfloat16)
    node_pre = jnp.dot(node_input, node_first, preferred_element_type=jnp.float32) + node_bias
    node_hidden = jax.nn.silu(node_pre).astype(jnp.bfloat16)
    node_out = jnp.dot(node_hidden, node_second, preferred_element_type=jnp.float32)
    new_latents = (owned + layer_norm(node_out, node_gain)).astype(jnp.bfloat16)
    return (new_latents, new_edges)


def local_step(
    latent_block, halo_block, edge_block, params, senders, receivers, edge_total, node_cot, edge_cot
):

    def forward(owned, halo_rows, edge_rows, weights):
        return local_layer(owned, halo_rows, edge_rows, weights, senders, receivers, edge_total)

    outputs, pullback = jax.vjp(
        forward,
        latent_block.astype(jnp.float32),
        halo_block.astype(jnp.float32),
        edge_block.astype(jnp.float32),
        params,
    )
    grad_owned, grad_halo, grad_edges, grad_params = pullback((node_cot, edge_cot))
    grad_params = tuple((item.astype(jnp.float32) for item in grad_params))
    return (outputs[0], grad_owned, grad_halo, grad_edges, grad_params)


def per_device(
    latents,
    stale_latents,
    edge_latents,
    senders,
    receivers,
    edge_count,
    send_list,
    node_cotangent,
    edge_cotangent,
    edge_first,
    edge_bias,
    edge_second,
    edge_gain,
    node_first,
    node_bias,
    node_second,
    node_gain,
):
    depth = send_list.shape[2]
    width = latents.shape[1]
    send_rows = send_list[0].reshape(-1)
    picked = jnp.take(stale_latents, send_rows, axis=0).reshape(4, depth, width)
    stream_pair = jnp.concatenate([picked[1], picked[0]], axis=0)
    cross_pair = jnp.concatenate([picked[3], picked[2]], axis=0)
    along = extended(stream_pair, (("stream", 0),), depth)
    across = extended(cross_pair, (("cross", 0),), depth)
    halo_rows = jnp.concatenate(
        [along[:depth], along[3 * depth :], across[:depth], across[3 * depth :]], axis=0
    )
    params = (
        edge_first,
        edge_bias,
        edge_second,
        edge_gain,
        node_first,
        node_bias,
        node_second,
        node_gain,
    )
    new_latents, grad_owned, grad_halo, grad_edges, grad_params = local_step(
        latents,
        halo_rows,
        edge_latents,
        params,
        senders,
        receivers,
        edge_count[0],
        node_cotangent,
        edge_cotangent,
    )
    halo_grads = grad_halo.reshape(4, depth, width)
    back_stream = extended(
        jnp.concatenate([halo_grads[0], halo_grads[1]], axis=0).astype(jnp.bfloat16),
        (("stream", 0),),
        depth,
    ).astype(jnp.float32)
    back_cross = extended(
        jnp.concatenate([halo_grads[2], halo_grads[3]], axis=0).astype(jnp.bfloat16),
        (("cross", 0),),
        depth,
    ).astype(jnp.float32)
    returned = jnp.concatenate(
        [
            back_stream[3 * depth :],
            back_stream[:depth],
            back_cross[3 * depth :],
            back_cross[:depth],
        ],
        axis=0,
    )
    stale_grads = (
        jnp.zeros(latents.shape, jnp.float32).at[send_rows].add(returned).astype(jnp.bfloat16)
    )
    entries = 0
    for item in grad_params:
        entries = entries + item.size
    limit = math.sqrt(entries)
    totals = lax.psum(grad_params, ("stream", "cross"))
    squares = jnp.zeros((), jnp.float32)
    for item in totals:
        squares = squares + jnp.sum(item * item)
    factor = jnp.minimum(1.0, limit * lax.rsqrt(squares))
    clipped = tuple((item * factor for item in totals))
    return (
        new_latents,
        grad_owned.astype(jnp.bfloat16),
        stale_grads,
        grad_edges.astype(jnp.bfloat16),
        clipped[0],
        clipped[1],
        clipped[2],
        clipped[3],
        clipped[4],
        clipped[5],
        clipped[6],
        clipped[7],
    )


def solution(mesh):
    in_specs = (
        P(("stream", "cross"), None),
        P(("stream", "cross"), None),
        P(("stream", "cross"), None),
        P(("stream", "cross")),
        P(("stream", "cross")),
        P(("stream", "cross")),
        P(("stream", "cross"), None, None),
        P(("stream", "cross"), None),
        P(("stream", "cross"), None),
        P(),
        P(),
        P(),
        P(),
        P(),
        P(),
        P(),
        P(),
    )
    out_specs = (
        P(("stream", "cross"), None),
        P(("stream", "cross"), None),
        P(("stream", "cross"), None),
        P(("stream", "cross"), None),
        P(),
        P(),
        P(),
        P(),
        P(),
        P(),
        P(),
        P(),
    )
    return jax.shard_map(
        per_device, mesh=mesh, in_specs=in_specs, out_specs=out_specs, check_vma=False
    )
```

profile of v0, /device:TPU:1, one launch (start us, length us, event | category | flops | bytes accessed | tf_op | source)
XLA Modules:
  0.0 495.8 jit_solution(1136352119721394524)
XLA Ops:
  10.8 5.6 %collective-permute-start = (bf16[128,128]{0,1:T(8,128)(2,1)S(1)}, bf16[128,128]{0,1:T(8,128)(2,1)S(1)}, u32[]{:S(2)}, u32[]{:S(2)}) collective-permute-start(bf16[128,128]{0,1:T(8,128)(2,1)S(1)} %get-tuple-element.66), channel_id=1, source_target_pairs={{0,16},{16,32},{32,48},{48,64},{64,80},{80,96},{96,112},{112,128},... | collective-permute-start | bytes 98312 | tf_op jit(solution)/shard_map/ppermute | solution.py:18
  17.7 4.0 collective-permute-start.2
  21.7 5.0 %collective-permute-start.1 = (bf16[128,128]{0,1:T(8,128)(2,1)S(1)}, bf16[128,128]{0,1:T(8,128)(2,1)S(1)}, u32[]{:S(2)}, u32[]{:S(2)}) collective-permute-start(bf16[128,128]{0,1:T(8,128)(2,1)S(1)} %get-tuple-element.69), channel_id=1, source_target_pairs={{16,0},{32,16},{48,32},{64,48},{80,64},{96,80},{112,96},{128,112},... | collective-permute-start | bytes 98312 | tf_op jit(solution)/shard_map/ppermute | solution.py:19
  31.6 3.2 gather_fusion.2
  35.7 3.2 gather_fusion.1
  42.0 9.1 %scatter_custom_fusion = f32[512,128]{1,0:T(8,128)S(1)} fusion(s32[1536]{0:T(1024)} %copy-done.24, f32[1536,128]{1,0:T(8,128)S(1)} %copy.54, f32[]{:T(128)} %constant.42.clone.1), kind=kCustom, calls=%fused_computation.89 | custom fusion | flops 196608 | bytes 262656 | tf_op jit(solution)/shard_map/jvp()/scatter-add | solution.py:49
  57.1 2.6 gather_fusion.3
  65.9 9.0 %scatter_custom_fusion.1 = f32[1024,128]{1,0:T(8,128)S(1)} fusion(s32[1536]{0:T(1024)} %copy-done.28, f32[1536,128]{1,0:T(8,128)S(1)} %copy.61, f32[]{:T(128)} %constant.42.clone.1), kind=kCustom, calls=%fused_computation.75 | custom fusion | flops 196608 | bytes 524800 | tf_op jit(solution)/shard_map/transpose(jvp(jit(_take)))/scatter-add | solution.py:36
  75.0 101.4 %all-reduce = (f32[128]{0:T(128)S(1)}, f32[128]{0:T(128)S(1)}, f32[128]{0:T(128)S(1)}, f32[128]{0:T(128)S(1)}) all-reduce(f32[128]{0:T(128)S(1)} %copy-done.38, f32[128]{0:T(128)S(1)} %copy-done.34, f32[128]{0:T(128)S(1)} %copy-done.37, f32[128]{0:T(128)S(1)} %copy-done.36), channel_id=1, replica_groups=mesh['stream'=32,'cross'=16] {'stream','cross'}, use_global_device_ids=true, to_apply=%region_15.16 | all-reduce | flops 512 | bytes 4096 | tf_op jit(solution)/shard_map/psum | solution.py:156
  179.8 4.0 collective-permute-start.6
  186.5 8.9 %scatter_fusion = f32[512,128]{1,0:T(8,128)S(1)} fusion(f32[512,128]{1,0:T(8,128)S(1)} %copy.63, s32[1536]{0:T(1024)S(1)} %copy-done.25, f32[1536,128]{1,0:T(8,128)S(1)} %copy.64), kind=kCustom, calls=%fused_computation.6 | custom fusion | flops 196608 | bytes 2365440 | tf_op jit(solution)/shard_map/transpose(jvp(jit(_take)))/scatter-add | solution.py:37
  196.1 5.3 %collective-permute-start.4 = (bf16[128,128]{1,0:T(8,128)(2,1)S(1)}, bf16[128,128]{1,0:T(8,128)(2,1)S(1)}, u32[]{:S(2)}, u32[]{:S(2)}) collective-permute-start(bf16[128,128]{1,0:T(8,128)(2,1)S(1)} %get-tuple-element.56), channel_id=1, source_target_pairs={{0,16},{16,32},{32,48},{48,64},{64,80},{80,96},{96,112},{112,128},... | collective-permute-start | bytes 98312 | tf_op jit(solution)/shard_map/ppermute | solution.py:18
  201.4 1.9 collective-permute-start.5
  203.4 4.1 collective-permute-done.5
  207.5 2.5 scatter_custom_fusion.3
  210.7 258.8 %all-reduce.4.cloned.1.call-done = (f32[384,128]{1,0:T(8,128)}, f32[128,128]{1,0:T(8,128)}, f32[256,128]{1,0:T(8,128)}, f32[128,128]{1,0:T(8,128)}) async-done(((f32[384,128]{1,0:T(8,128)}, f32[128,128]{1,0:T(8,128)}, f32[256,128]{1,0:T(8,128)}, f32[128,128]{1,0:T(8,128)}), (f32[384,128]{1,0:T(8,128)}, f32[128,128]{1,0:T(8,128)}, f32[256,128]{1,0:T(8,128)}, ...) | async-done | bytes 458768 | tf_op jit(solution)/shard_map/psum | solution.py:156
  469.5 1.5 multiply_reduce_fusion.4
  470.9 1.5 multiply_reduce_fusion.3
  472.5 1.5 multiply_reduce_fusion.5
  473.9 1.6 multiply_reduce_fusion.2
  482.3 1.5 broadcast_multiply_fusion.2
  483.8 1.6 broadcast_multiply_fusion.1
  485.4 1.5 broadcast_multiply_fusion.3
  487.4 1.6 broadcast_multiply_fusion
  (176 shorter events, 34.1 us)
Async XLA Ops:
  7.2 24.1 %copy-start.5 = (bf16[512,128]{1,0:T(8,128)(2,1)S(1)}, bf16[512,128]{1,0:T(8,128)(2,1)}, u32[]{:S(2)}) copy-start(bf16[512,128]{1,0:T(8,128)(2,1)} %param.17) | copy-start | bytes 393220
  7.2 462.3 %all-reduce.4.cloned.1.call-start = ((), (), s32[]{:S(2)}) async-start(), calls=%async_computation | async-start | bytes 917504 | tf_op jit(solution)/shard_map/psum | solution.py:156
  10.8 24.6 %collective-permute-start = (bf16[128,128]{0,1:T(8,128)(2,1)S(1)}, bf16[128,128]{0,1:T(8,128)(2,1)S(1)}, u32[]{:S(2)}, u32[]{:S(2)}) collective-permute-start(bf16[128,128]{0,1:T(8,128)(2,1)S(1)} %get-tuple-element.66), channel_id=1, source_target_pairs={{0,16},{16,32},{32,48},{48,64},{64,80},{80,96},{96,112},{112,128},... | collective-permute-start | bytes 98312 | tf_op jit(solution)/shard_map/ppermute | solution.py:18
  16.4 19.0 %collective-permute-start.3 = (bf16[128,128]{0,1:T(8,128)(2,1)S(1)}, bf16[128,128]{0,1:T(8,128)(2,1)S(1)}, u32[]{:S(2)}, u32[]{:S(2)}) collective-permute-start(bf16[128,128]{0,1:T(8,128)(2,1)S(1)} %get-tuple-element.67), channel_id=1, source_target_pairs={{1,0},{2,1},{3,2},{4,3},{5,4},{6,5},{7,6},{8,7},{9,8},{10,9},{11,1... | collective-permute-start | bytes 98312 | tf_op jit(solution)/shard_map/ppermute | solution.py:19
  17.7 17.7 %collective-permute-start.2 = (bf16[128,128]{0,1:T(8,128)(2,1)S(1)}, bf16[128,128]{0,1:T(8,128)(2,1)S(1)}, u32[]{:S(2)}, u32[]{:S(2)}) collective-permute-start(bf16[128,128]{0,1:T(8,128)(2,1)S(1)} %get-tuple-element.68), channel_id=1, source_target_pairs={{0,1},{1,2},{2,3},{3,4},{4,5},{5,6},{6,7},{7,8},{8,9},{9,10},{10,1... | collective-permute-start | bytes 98312 | tf_op jit(solution)/shard_map/ppermute | solution.py:18
  21.7 13.7 %collective-permute-start.1 = (bf16[128,128]{0,1:T(8,128)(2,1)S(1)}, bf16[128,128]{0,1:T(8,128)(2,1)S(1)}, u32[]{:S(2)}, u32[]{:S(2)}) collective-permute-start(bf16[128,128]{0,1:T(8,128)(2,1)S(1)} %get-tuple-element.69), channel_id=1, source_target_pairs={{16,0},{32,16},{48,32},{64,48},{80,64},{96,80},{112,96},{128,112},... | collective-permute-start | bytes 98312 | tf_op jit(solution)/shard_map/ppermute | solution.py:19
  27.4 11.6 %copy-start.29 = (pred[1536]{0:T(1024)(128)(4,1)}, pred[1536]{0:T(1024)(128)(4,1)S(1)}, u32[]{:S(2)}) copy-start(pred[1536]{0:T(1024)(128)(4,1)S(1)} %compare_and_fusion) | copy-start | bytes 4612
  41.1 10.1 %copy-start.15 = (bf16[256,128]{1,0:T(8,128)(2,1)S(1)}, bf16[256,128]{1,0:T(8,128)(2,1)}, u32[]{:S(2)}) copy-start(bf16[256,128]{1,0:T(8,128)(2,1)} %param.30) | copy-start | bytes 196612
  41.1 10.1 %copy-start.39 = (f32[128]{0:T(128)S(1)}, f32[128]{0:T(128)}, u32[]{:S(2)}) copy-start(f32[128]{0:T(128)} %param.31) | copy-start | bytes 1540
  41.5 9.9 %copy-start.20 = (f32[1536]{0:T(1024)}, f32[1536]{0:T(1024)S(1)}, u32[]{:S(2)}) copy-start(f32[1536]{0:T(1024)S(1)} %multiply_reduce_fusion) | copy-start | bytes 18436
  41.5 9.9 %copy-start.18 = (f32[1536]{0:T(1024)}, f32[1536]{0:T(1024)S(1)}, u32[]{:S(2)}) copy-start(f32[1536]{0:T(1024)S(1)} %fusion.49) | copy-start | bytes 18436
  41.5 9.9 %copy-start.40 = (bf16[128,128]{1,0:T(8,128)(2,1)S(1)}, bf16[128,128]{1,0:T(8,128)(2,1)}, u32[]{:S(2)}) copy-start(bf16[128,128]{1,0:T(8,128)(2,1)} %param.32) | copy-start | bytes 98308
  41.8 10.0 %copy-start.35 = (f32[128]{0:T(128)S(1)}, f32[128]{0:T(128)}, u32[]{:S(2)}) copy-start(f32[128]{0:T(128)} %param.33) | copy-start | bytes 1540
  65.5 9.5 %copy-start.34 = (f32[128]{0:T(128)S(1)}, f32[128]{0:T(128)}, u32[]{:S(2)}) copy-start(f32[128]{0:T(128)} %get-tuple-element.36) | copy-start | bytes 1540
  65.5 9.5 %copy-start.36 = (f32[128]{0:T(128)S(1)}, f32[128]{0:T(128)}, u32[]{:S(2)}) copy-start(f32[128]{0:T(128)} %get-tuple-element.38) | copy-start | bytes 1540
  65.6 9.4 %copy-start.37 = (f32[128]{0:T(128)S(1)}, f32[128]{0:T(128)}, u32[]{:S(2)}) copy-start(f32[128]{0:T(128)} %get-tuple-element.80) | copy-start | bytes 1540
  65.6 9.4 %copy-start.38 = (f32[128]{0:T(128)S(1)}, f32[128]{0:T(128)}, u32[]{:S(2)}) copy-start(f32[128]{0:T(128)} %get-tuple-element.78) | copy-start | bytes 1540
  65.6 112.9 %copy-start.2 = (f32[512,256]{0,1:T(8,128)S(1)}, f32[512,256]{0,1:T(8,128)}, u32[]{:S(2)}) copy-start(f32[512,256]{0,1:T(8,128)} %copy-done.1) | copy-start | bytes 1572868
  74.9 109.6 %copy-start.6 = (bf16[512,128]{0,1:T(8,128)(2,1)S(1)}, bf16[512,128]{0,1:T(8,128)(2,1)}, u32[]{:S(2)}) copy-start(bf16[512,128]{0,1:T(8,128)(2,1)} %get-tuple-element.55) | copy-start | bytes 393220
  75.0 111.5 %copy-start.25 = (s32[1536]{0:T(1024)S(1)}, s32[1536]{0:T(1024)}, u32[]{:S(2)}) copy-start(s32[1536]{0:T(1024)} %copy-done.24) | copy-start | bytes 18436
  178.5 24.8 %collective-permute-start.7 = (bf16[128,128]{1,0:T(8,128)(2,1)S(1)}, bf16[128,128]{1,0:T(8,128)(2,1)S(1)}, u32[]{:S(2)}, u32[]{:S(2)}) collective-permute-start(bf16[128,128]{1,0:T(8,128)(2,1)S(1)} %get-tuple-element.57), channel_id=1, source_target_pairs={{1,0},{2,1},{3,2},{4,3},{5,4},{6,5},{7,6},{8,7},{9,8},{10,9},{11,1... | collective-permute-start | bytes 98312 | tf_op jit(solution)/shard_map/ppermute | solution.py:19
  179.8 23.5 %collective-permute-start.6 = (bf16[128,128]{1,0:T(8,128)(2,1)S(1)}, bf16[128,128]{1,0:T(8,128)(2,1)S(1)}, u32[]{:S(2)}, u32[]{:S(2)}) collective-permute-start(bf16[128,128]{1,0:T(8,128)(2,1)S(1)} %get-tuple-element.58), channel_id=1, source_target_pairs={{0,1},{1,2},{2,3},{3,4},{4,5},{5,6},{6,7},{7,8},{8,9},{9,10},{10,1... | collective-permute-start | bytes 98312 | tf_op jit(solution)/shard_map/ppermute | solution.py:18
  196.1 7.3 %collective-permute-start.4 = (bf16[128,128]{1,0:T(8,128)(2,1)S(1)}, bf16[128,128]{1,0:T(8,128)(2,1)S(1)}, u32[]{:S(2)}, u32[]{:S(2)}) collective-permute-start(bf16[128,128]{1,0:T(8,128)(2,1)S(1)} %get-tuple-element.56), channel_id=1, source_target_pairs={{0,16},{16,32},{32,48},{48,64},{64,80},{80,96},{96,112},{112,128},... | collective-permute-start | bytes 98312 | tf_op jit(solution)/shard_map/ppermute | solution.py:18
  201.4 6.1 %collective-permute-start.5 = (bf16[128,128]{1,0:T(8,128)(2,1)S(1)}, bf16[128,128]{1,0:T(8,128)(2,1)S(1)}, u32[]{:S(2)}, u32[]{:S(2)}) collective-permute-start(bf16[128,128]{1,0:T(8,128)(2,1)S(1)} %get-tuple-element.59), channel_id=1, source_target_pairs={{16,0},{32,16},{48,32},{64,48},{80,64},{96,80},{112,96},{128,112},... | collective-permute-start | bytes 98312 | tf_op jit(solution)/shard_map/ppermute | solution.py:19
  (28 other events, 64.9 us)
Sparse Core Ops, SparseCore 0:
  203.5 265.9 all-reduce.3
where the time goes:
time: 497 us; the launch traced here: 496 us
  waiting for transfers between devices  263 us (53%)
  blocking collectives  101 us (20%)
  other arithmetic  55.3 us (11%)
  starting transfers between devices  28.5 us (6%)
  between operations  21 us (4%)
  local copies, waits for them, and re-layouts  17.7 us (4%)
  matrix products  9 us (2%)
    psum x1, waiting for transfers between devices, per_device(): totals = lax.psum(grad_params, ('stream', 'cross'))  259 us
    psum x1, blocking collectives, per_device(): totals = lax.psum(grad_params, ('stream', 'cross'))  101 us
    ppermute x4, starting transfers between devices, extended(): before = lax.ppermute(last, axis, up)  18.9 us
  transfers between devices with their start and end apart: 9, of which 2 were waited for; matrix products, arithmetic and copies ran while one was open for 5% of the time, Pallas kernels for 0%

commit v1 on v0

v1 whole, which is shorter than its diff:
```python
import math

import jax
import jax.numpy as jnp
from jax import lax
from jax.experimental import pallas as pl
from jax.experimental.pallas import tpu as pltpu
from jax.sharding import PartitionSpec as P

EPSILON = 1e-05
MESH = pl.DeviceIdType.MESH
F32 = jnp.float32
BF16 = jnp.bfloat16
W = 128
NODES = 512
EDGES = 1536
HALO = 128
CHUNK = 256
TILE = 32
NEAR = 32
FAR = 16
PACK = TILE * NEAR
ROW_NODE_FIRST = 0
ROW_NODE_SECOND = 256
ROW_EDGE_SECOND = 384
ROW_EDGE_FIRST = 512
ROW_SMALL = 896

CORE = ("s", 1, 2)
Y_HI = ("s", 2, 4)
X = ("s", 8, 4)
Y_LO = ("c", 1, 2)
Z_0 = ("c", 2, 2)
Z_HI = ("c", 4, 4)


class Group:
    def __init__(self, digits, s, c):
        self.s, self.c = s, c
        self.pos = 0
        self.peers = [(0, 0, 0, 0)]
        size = 1
        for axis, stride, n in digits:
            d = ((s if axis == "s" else c) // stride) % n
            self.pos = self.pos + d * size
            grown = []
            for k in range(n):
                q = (d + k) % n if k else d
                step = (q - d) * stride if k else 0
                for key, ds, dc, at in self.peers:
                    grown.append(
                        (
                            key + k * size,
                            ds + step if axis == "s" else ds,
                            dc + step if axis == "c" else dc,
                            at + q * size,
                        )
                    )
            self.peers = grown
            size *= n
        self.size = size
        self.peers = sorted(self.peers, key=lambda p: p[0])[1:]

    def others(self):
        for key, ds, dc, at in self.peers:
            yield key, (self.s + ds, self.c + dc), at


def dot(a, b):
    return jnp.dot(a, b, preferred_element_type=F32)


def dot_nt(a, b):
    return lax.dot_general(a, b, (((1,), (1,)), ((), ())), preferred_element_type=F32)


def dot_tn(a, b):
    return lax.dot_general(a, b, (((0,), (0,)), ((), ())), preferred_element_type=F32)


def columns_of(ref, first, count):
    parts = []
    for k in range(count):
        row = ref[pl.ds(first + k, 1), :]
        parts.append(jnp.broadcast_to(row, (W, W)).T)
    return parts[0] if count == 1 else jnp.concatenate(parts, axis=0)


def hot_rows(col, blocks):
    lane = lax.broadcasted_iota(jnp.int32, col.shape, 1)
    return jnp.concatenate(
        [jnp.where(col == lane + W * j, 1.0, 0.0).astype(BF16) for j in range(blocks)], axis=1
    )


def hot_cols(row, height):
    at = lax.broadcasted_iota(jnp.int32, (height, row.shape[1]), 0)
    return jnp.where(at == row, 1.0, 0.0).astype(BF16)


def sigmoid(v):
    return 0.5 * jnp.tanh(0.5 * v) + 0.5


def normed(z):
    centered = z - jnp.mean(z, axis=-1, keepdims=True)
    rstd = lax.rsqrt(jnp.mean(centered * centered, axis=-1, keepdims=True) + EPSILON)
    return centered * rstd, rstd


def normed_back(dx, xhat, rstd):
    m1 = jnp.mean(dx, axis=-1, keepdims=True)
    m2 = jnp.mean(dx * xhat, axis=-1, keepdims=True)
    return rstd * (dx - m1 - xhat * m2)


def place():
    s = lax.axis_index("stream")
    c = lax.axis_index("cross")
    ns = lax.axis_size("stream")
    nc = lax.axis_size("cross")
    to = [((s + 1, c), s < ns - 1), ((s - 1, c), s > 0), ((s, c + 1), c < nc - 1), ((s, c - 1), c > 0)]
    count = sum(ok.astype(jnp.int32) for _, ok in to)
    return s, c, to, count


BACK = (1, 0, 3, 2)


def halo_kernel(stale_ref, list_ref, halo_ref, picked, landed, send_sem, recv_sem):
    s, c, to, count = place()
    barrier = pltpu.get_barrier_semaphore()
    for where, ok in to:

        @pl.when(ok)
        def _(where=where):
            pl.semaphore_signal(barrier, inc=1, device_id=where, device_id_type=MESH)

    table = jnp.concatenate([stale_ref[:256, :], stale_ref[256:, :]], axis=1)
    for k in range(4):
        col = columns_of(list_ref, k, 1)
        both = dot(hot_rows(col & 255, 2), table)
        picked[k] = jnp.where(col < 256, both[:, :W], both[:, W:]).astype(BF16)

    pl.semaphore_wait(barrier, count)

    def copy(k):
        return pltpu.make_async_remote_copy(
            src_ref=picked.at[k],
            dst_ref=landed.at[k],
            send_sem=send_sem.at[k],
            recv_sem=recv_sem.at[k],
            device_id=to[k][0],
            device_id_type=MESH,
        )

    for k in range(4):

        @pl.when(to[k][1])
        def _(k=k):
            copy(k).start()

    for k in range(4):
        has = to[BACK[k]][1]

        @pl.when(has)
        def _(k=k):
            copy(k).wait_recv()
            halo_ref[HALO * k : HALO * (k + 1), :] = landed[k]

        @pl.when(jnp.logical_not(has))
        def _(k=k):
            halo_ref[HALO * k : HALO * (k + 1), :] = jnp.zeros((HALO, W), BF16)

    for k in range(4):

        @pl.when(to[k][1])
        def _(k=k):
            copy(k).wait_send()


def layer_kernel(
    lat_ref,
    halo_ref,
    edge_ref,
    snd_ref,
    rcv_ref,
    count_ref,
    list_ref,
    ncot_ref,
    ecot_ref,
    w1_ref,
    b1_ref,
    w2_ref,
    g_ref,
    nw1_ref,
    nb1_ref,
    nw2_ref,
    ng_ref,
    new_ref,
    latg_ref,
    staleg_ref,
    edgeg_ref,
    gw1_ref,
    gb1_ref,
    gw2_ref,
    gg_ref,
    gnw1_ref,
    gnb1_ref,
    gnw2_ref,
    gng_ref,
    hot_r,
    rows_sr,
    hidden,
    slope,
    xhat_s,
    rstd_s,
    values,
    d_pre,
    pack,
    near_in,
    near_sum,
    far_in,
    far_sum,
    total,
    halo_out,
    halo_in,
    near_send,
    near_recv,
    far_send,
    far_recv,
    all_send,
    all_recv,
    halo_send,
    halo_recv,
):
    s, c, to, count = place()
    near = Group((CORE, X, Y_LO, Z_0), s, c)
    far = Group((Y_HI, Z_HI), s, c)
    barrier = pltpu.get_barrier_semaphore()
    for where, ok in to:

        @pl.when(ok)
        def _(where=where):
            pl.semaphore_signal(barrier, inc=1, device_id=where, device_id_type=MESH)

    for group in (far, near):
        for _, where, _ in group.others():
            pl.semaphore_signal(barrier, inc=1, device_id=where, device_id_type=MESH)

    alive_count = count_ref[0]
    lat = lat_ref[...]
    table_s = jnp.concatenate([lat, halo_ref[...]], axis=1)
    table_r = jnp.concatenate([lat[:256, :], lat[256:, :]], axis=1)
    gain = g_ref[...]
    per = CHUNK // W

    def alive_rows(i):
        at = lax.broadcasted_iota(jnp.int32, (CHUNK, W), 0) + i * CHUNK
        return at < alive_count

    def forward(i, carry):
        at = pl.ds(pl.multiple_of(i * CHUNK, CHUNK), CHUNK)
        col_s = columns_of(snd_ref, i * per, per)
        col_r = columns_of(rcv_ref, i * per, per)
        alive = alive_rows(i)
        both = dot(hot_rows(col_s & 511, 4), table_s)
        rows_s = jnp.where(col_s < 512, both[:, :W], both[:, W:]).astype(BF16)
        hot = hot_rows(jnp.where(alive, col_r & 255, -1), 2)
        hot_r[at, :] = hot
        both = dot(hot, table_r)
        low = col_r < 256
        rows_r = jnp.where(low, both[:, :W], both[:, W:]).astype(BF16)
        edge = edge_ref[at, :]
        joined = jnp.concatenate([edge, rows_s, rows_r], axis=1)
        rows_sr[at, :] = joined
        pre = dot(joined, w1_ref[...]) + b1_ref[...]
        gate = sigmoid(pre)
        act = pre * gate
        slope[at, :] = gate + act * (1.0 - gate)
        act = act.astype(BF16)
        hidden[at, :] = act
        xhat, rstd = normed(dot(act, w2_ref[...]))
        xhat_s[at, :] = xhat
        rstd_s[at, :] = jnp.broadcast_to(rstd, xhat.shape)
        new = edge.astype(F32) + xhat * gain
        values[at, :] = jnp.concatenate(
            [jnp.where(low, new, 0.0).astype(BF16), jnp.where(low, 0.0, new).astype(BF16)], axis=1
        )
        return carry

    lax.fori_loop(0, EDGES // CHUNK, forward, 0)

    def masked_receivers():
        at = lax.broadcasted_iota(jnp.int32, (1, W), 1)
        rows = []
        for k in range(EDGES // W):
            rows.append(jnp.where(at + k * W < alive_count, rcv_ref[k : k + 1, :] & 255, -1))
        return jnp.concatenate(rows, axis=1)

    hot_rt = hot_cols(masked_receivers(), 256)
    agg = dot(hot_rt, values[...])
    agg = jnp.concatenate([agg[:, :W], agg[:, W:]], axis=0).astype(BF16)

    node_in = jnp.concatenate([lat, agg], axis=1)
    pre = dot(node_in, nw1_ref[...]) + nb1_ref[...]
    gate = sigmoid(pre)
    act = pre * gate
    node_slope = gate + act * (1.0 - gate)
    act = act.astype(BF16)
    xhat, rstd = normed(dot(act, nw2_ref[...]))
    ngain = ng_ref[...]
    new_ref[...] = (lat.astype(F32) + xhat * ngain).astype(BF16)
    dy = ncot_ref[...].astype(F32)
    d_ngain = jnp.sum(dy * xhat, axis=0, keepdims=True)
    dz = normed_back(dy * ngain, xhat, rstd).astype(BF16)
    pack[ROW_NODE_SECOND : ROW_NODE_SECOND + 128, :] = dot_tn(act, dz).astype(BF16)
    dp = dot_nt(dz, nw2_ref[...]) * node_slope
    d_nbias = jnp.sum(dp, axis=0, keepdims=True)
    dp = dp.astype(BF16)
    pack[ROW_NODE_FIRST : ROW_NODE_FIRST + 256, :] = dot_tn(node_in, dp).astype(BF16)
    d_in = dot_nt(dp, nw1_ref[...])
    own = dy + d_in[:, :W]
    d_agg = d_in[:, W:].astype(BF16)
    table_d = jnp.concatenate([d_agg[:256, :], d_agg[256:, :]], axis=1)

    def backward(i, carry):
        d_gain, d_bias = carry
        at = pl.ds(pl.multiple_of(i * CHUNK, CHUNK), CHUNK)
        col_r = columns_of(rcv_ref, i * per, per)
        both = dot(hot_r[at, :], table_d)
        ct = ecot_ref[at, :].astype(F32) + jnp.where(col_r < 256, both[:, :W], both[:, W:])
        dy = jnp.where(alive_rows(i), ct, 0.0)
        xhat = xhat_s[at, :]
        d_gain = d_gain + jnp.sum(dy * xhat, axis=0, keepdims=True)
        dz = normed_back(dy * gain, xhat, rstd_s[at, :]).astype(BF16)
        dp = dot_nt(dz, w2_ref[...]) * slope[at, :]
        d_bias = d_bias + jnp.sum(dp, axis=0, keepdims=True)
        d_pre[at, :] = dp.astype(BF16)
        xhat_s[at, :] = ct
        values[at, :W] = dz
        return d_gain, d_bias

    zero = jnp.zeros((1, W), F32)
    d_gain, d_bias = lax.fori_loop(0, EDGES // CHUNK, backward, (zero, zero))
    pack[ROW_EDGE_SECOND : ROW_EDGE_SECOND + 128, :] = dot_tn(hidden[...], values[:, :W]).astype(BF16)
    pack[ROW_EDGE_FIRST : ROW_EDGE_FIRST + 384, :] = dot_tn(rows_sr[...], d_pre[...]).astype(BF16)
    pack[ROW_SMALL:, :] = jnp.concatenate(
        [d_bias, d_gain, d_nbias, d_ngain, jnp.zeros((PACK - ROW_SMALL - 4, W), F32)], axis=0
    ).astype(BF16)

    pl.semaphore_wait(barrier, count + (NEAR - 1) + (FAR - 1))
    for key, where, at in near.others():
        pltpu.make_async_remote_copy(
            src_ref=pack.at[pl.ds(pl.multiple_of(at * TILE, TILE), TILE)],
            dst_ref=near_in.at[key - 1],
            send_sem=near_send,
            recv_sem=near_recv,
            device_id=where,
            device_id_type=MESH,
        ).start()

    def spread(i, carry):
        at = pl.ds(pl.multiple_of(i * CHUNK, CHUNK), CHUNK)
        d_joined = dot_nt(d_pre[at, :], w1_ref[...])
        edgeg_ref[at, :] = (xhat_s[at, :] + d_joined[:, :W]).astype(BF16)
        mine = columns_of(snd_ref, i * per, per) < 512
        d_s = d_joined[:, W : 2 * W]
        values[at, :] = jnp.concatenate(
            [jnp.where(mine, d_s, 0.0).astype(BF16), jnp.where(mine, 0.0, d_s).astype(BF16)], axis=1
        )
        low = columns_of(rcv_ref, i * per, per) < 256
        d_r = d_joined[:, 2 * W :]
        rows_sr[at, : 2 * W] = jnp.concatenate(
            [jnp.where(low, d_r, 0.0).astype(BF16), jnp.where(low, 0.0, d_r).astype(BF16)], axis=1
        )
        return carry

    lax.fori_loop(0, EDGES // CHUNK, spread, 0)
    senders = jnp.concatenate([snd_ref[k : k + 1, :] & 511 for k in range(EDGES // W)], axis=1)
    spread_s = dot(hot_cols(senders, 512), values[...])
    for k in range(4):
        halo_out[k] = spread_s[HALO * k : HALO * (k + 1), W:].astype(BF16)

    def back(k):
        return pltpu.make_async_remote_copy(
            src_ref=halo_out.at[k],
            dst_ref=halo_in.at[k],
            send_sem=halo_send.at[k],
            recv_sem=halo_recv.at[k],
            device_id=to[BACK[k]][0],
            device_id_type=MESH,
        )

    for k in range(4):

        @pl.when(to[BACK[k]][1])
        def _(k=k):
            back(k).start()

    spread_r = dot(hot_cols(masked_receivers(), 256), rows_sr[:, : 2 * W])
    latg_ref[...] = (
        own + spread_s[:, :W] + jnp.concatenate([spread_r[:, :W], spread_r[:, W:]], axis=0)
    ).astype(BF16)

    mine = pl.ds(pl.multiple_of(near.pos * TILE, TILE), TILE)
    pltpu.make_async_copy(near_in, near_in, near_recv).wait()
    acc = pack[mine, :].astype(F32)
    for k in range(NEAR - 1):
        acc = acc + near_in[k].astype(F32)
    near_sum[...] = acc.astype(BF16)
    for key, where, at in far.others():
        pltpu.make_async_remote_copy(
            src_ref=near_sum,
            dst_ref=far_in.at[far.pos],
            send_sem=far_send,
            recv_sem=far_recv,
            device_id=where,
            device_id_type=MESH,
        ).start()

    for k in range(4):
        has = to[k][1]

        @pl.when(has)
        def _(k=k):
            back(k).wait_recv()

        @pl.when(jnp.logical_not(has))
        def _(k=k):
            halo_in[k] = jnp.zeros((HALO, W), BF16)

    parts = []
    for k in range(4):
        low = columns_of(list_ref, k, 1) < 256
        came = halo_in[k].astype(F32)
        parts.append(
            jnp.concatenate(
                [jnp.where(low, came, 0.0).astype(BF16), jnp.where(low, 0.0, came).astype(BF16)],
                axis=1,
            )
        )
    listed = jnp.concatenate([list_ref[k : k + 1, :] & 255 for k in range(4)], axis=1)
    stale = dot(hot_cols(listed, 256), jnp.concatenate(parts, axis=0))
    staleg_ref[...] = jnp.concatenate([stale[:, :W], stale[:, W:]], axis=0).astype(BF16)

    pltpu.make_async_copy(far_in.at[pl.ds(0, FAR - 1)], far_in.at[pl.ds(0, FAR - 1)], far_recv).wait()
    far_in[far.pos] = near_sum[...]
    acc = far_in[0].astype(F32)
    for k in range(1, FAR):
        acc = acc + far_in[k].astype(F32)
    far_sum[...] = acc.astype(BF16)
    for key, where, at in near.others():
        pltpu.make_async_remote_copy(
            src_ref=far_sum,
            dst_ref=total.at[mine],
            send_sem=all_send,
            recv_sem=all_recv,
            device_id=where,
            device_id_type=MESH,
        ).start()
    rest = total.at[pl.ds(0, PACK - TILE)]
    pltpu.make_async_copy(rest, rest, all_recv).wait()
    total[mine, :] = far_sum[...]
    sums = total[...].astype(F32)
    entries = ROW_SMALL * W + 4 * W
    squares = jnp.sum(sums * sums)
    factor = jnp.minimum(1.0, math.sqrt(entries) * lax.rsqrt(jnp.full((1, W), squares, F32)))
    sums = sums * factor
    gnw1_ref[...] = sums[ROW_NODE_FIRST : ROW_NODE_FIRST + 256, :]
    gnw2_ref[...] = sums[ROW_NODE_SECOND : ROW_NODE_SECOND + 128, :]
    gw2_ref[...] = sums[ROW_EDGE_SECOND : ROW_EDGE_SECOND + 128, :]
    gw1_ref[...] = sums[ROW_EDGE_FIRST : ROW_EDGE_FIRST + 384, :]
    gb1_ref[...] = sums[ROW_SMALL : ROW_SMALL + 1, :]
    gg_ref[...] = sums[ROW_SMALL + 1 : ROW_SMALL + 2, :]
    gnb1_ref[...] = sums[ROW_SMALL + 2 : ROW_SMALL + 3, :]
    gng_ref[...] = sums[ROW_SMALL + 3 : ROW_SMALL + 4, :]

    for k in range(4):

        @pl.when(to[BACK[k]][1])
        def _(k=k):
            back(k).wait_send()

    pltpu.make_async_copy(near_in, near_in, near_send).wait()
    pltpu.make_async_copy(far_in.at[pl.ds(0, FAR - 1)], far_in.at[pl.ds(0, FAR - 1)], far_send).wait()
    pltpu.make_async_copy(rest, rest, all_send).wait()


def per_device(
    latents,
    stale_latents,
    edge_latents,
    senders,
    receivers,
    edge_count,
    send_list,
    node_cotangent,
    edge_cotangent,
    edge_first,
    edge_bias,
    edge_second,
    edge_gain,
    node_first,
    node_bias,
    node_second,
    node_gain,
):
    vmem = pl.BlockSpec(memory_space=pltpu.VMEM)
    smem = pl.BlockSpec(memory_space=pltpu.SMEM)
    listed = send_list[0]
    halo = pl.pallas_call(
        halo_kernel,
        out_shape=jax.ShapeDtypeStruct((4 * HALO, W), BF16),
        in_specs=[vmem, vmem],
        out_specs=vmem,
        scratch_shapes=[
            pltpu.VMEM((4, HALO, W), BF16),
            pltpu.VMEM((4, HALO, W), BF16),
            pltpu.SemaphoreType.DMA((4,)),
            pltpu.SemaphoreType.DMA((4,)),
        ],
        compiler_params=pltpu.CompilerParams(
            collective_id=0, has_side_effects=True, vmem_limit_bytes=16 * 2**20
        ),
    )(stale_latents, listed)

    def row(v):
        return v.reshape(1, W)

    def shape(rows, dtype):
        return jax.ShapeDtypeStruct((rows, W), dtype)

    outs = pl.pallas_call(
        layer_kernel,
        out_shape=(
            shape(NODES, BF16),
            shape(NODES, BF16),
            shape(NODES, BF16),
            shape(EDGES, BF16),
            shape(384, F32),
            shape(1, F32),
            shape(128, F32),
            shape(1, F32),
            shape(256, F32),
            shape(1, F32),
            shape(128, F32),
            shape(1, F32),
        ),
        in_specs=[vmem] * 5 + [smem] + [vmem] * 11,
        out_specs=(vmem,) * 12,
        scratch_shapes=[
            pltpu.VMEM((EDGES, 256), BF16),
            pltpu.VMEM((EDGES, 384), BF16),
            pltpu.VMEM((EDGES, W), BF16),
            pltpu.VMEM((EDGES, W), F32),
            pltpu.VMEM((EDGES, W), F32),
            pltpu.VMEM((EDGES, W), F32),
            pltpu.VMEM((EDGES, 256), BF16),
            pltpu.VMEM((EDGES, W), BF16),
            pltpu.VMEM((PACK, W), BF16),
            pltpu.VMEM((NEAR - 1, TILE, W), BF16),
            pltpu.VMEM((TILE, W), BF16),
            pltpu.VMEM((FAR, TILE, W), BF16),
            pltpu.VMEM((TILE, W), BF16),
            pltpu.VMEM((PACK, W), BF16),
            pltpu.VMEM((4, HALO, W), BF16),
            pltpu.VMEM((4, HALO, W), BF16),
        ]
        + [pltpu.SemaphoreType.DMA] * 6
        + [pltpu.SemaphoreType.DMA((4,))] * 2,
        compiler_params=pltpu.CompilerParams(
            collective_id=1, has_side_effects=True, vmem_limit_bytes=48 * 2**20
        ),
    )(
        latents,
        halo,
        edge_latents,
        senders.reshape(EDGES // W, W),
        receivers.reshape(EDGES // W, W),
        edge_count,
        listed,
        node_cotangent,
        edge_cotangent,
        edge_first,
        row(edge_bias),
        edge_second,
        row(edge_gain),
        node_first,
        row(node_bias),
        node_second,
        row(node_gain),
    )
    return tuple(v.reshape(W) if v.shape[0] == 1 else v for v in outs)


def solution(mesh):
    both = ("stream", "cross")
    rows = P(both, None)
    in_specs = (rows, rows, rows, P(both), P(both), P(both), P(both, None, None), rows, rows) + (P(),) * 8
    out_specs = (rows,) * 4 + (P(),) * 8
    return jax.shard_map(
        per_device, mesh=mesh, in_specs=in_specs, out_specs=out_specs, check_vma=False
    )
```

time: 497 us -> 66.2 us (0.13)
  waiting for transfers between devices: 263 us -> 0 us
  blocking collectives: 101 us -> 0 us
  other arithmetic: 55.3 us -> 0 us
  Pallas kernels: 0 us -> 49.3 us
  starting transfers between devices: 28.5 us -> 0 us
  between operations: 21 us -> 1.42 us
  matrix products: 9 us -> 0 us
    psum x1 -> x0, waiting for transfers between devices: 259 us -> none  [per_device(): totals = lax.psum(grad_params, ('stream', 'cross'))]
    psum x1 -> x0, blocking collectives: 101 us -> none  [per_device(): totals = lax.psum(grad_params, ('stream', 'cross'))]
    pallas_call x0 -> x2, Pallas kernels: none -> 49.3 us  [the longest x1 39.8 us: per_device(): pl.pallas_call(layer_kernel, out_shape=(shape(NODES, BF16), shape(NODES,...]
    scatter-add x4 -> x0, other arithmetic: 29.4 us -> none  [the longest x1 9.11 us: local_layer(): summed = jnp.zeros(owned.shape, jnp.float32).at[receivers].add(edge_alive...]
    ppermute x8 -> x0, starting transfers between devices: 28.4 us -> none  [the longest x4 18.9 us: extended(): before = lax.ppermute(last, axis, up)]
    reduce_sum x13 -> x0, other arithmetic: 11.3 us -> none  [the longest x8 8.58 us: per_device(): squares = squares + jnp.sum(item * item)]
    gather x8 -> x0, local copies, waits for them, and re-layouts: 11.1 us -> none  [the longest x2 3.39 us: local_layer(): sender_rows = jnp.take(node_table, senders, axis=0)]
    unnamed x93 -> x44, local copies, waits for them, and re-layouts: 5.27 us -> 14.9 us
  transfers between devices with their start and end apart: 9 -> 0, of which waited for: 2 -> 0; matrix products, arithmetic and copies ran while one was open for 5% -> 0% of each run, Pallas kernels for 0% -> 0%
where the time goes in v1:
time: 66.2 us; the launch traced here: 65.6 us
  Pallas kernels  49.3 us (74%)
  local copies, waits for them, and re-layouts  14.9 us (23%)
  between operations  1.42 us (2%)
    pallas_call x1, Pallas kernels, per_device(): pl.pallas_call(layer_kernel, out_shape=(shape(NODES, BF16), shape(NODES,...  39.8 us
    unnamed x44, local copies, waits for them, and re-layouts  14.9 us
    pallas_call x1, Pallas kernels, per_device(): pl.pallas_call(halo_kernel, out_shape=jax.ShapeDtypeStruct((4 * HALO, W),...  9.49 us

profile of v1, /device:TPU:1, one launch (start us, length us, event | category | flops | bytes accessed | tf_op | source)
XLA Modules:
  0.0 65.6 jit_solution(11120420568955818816)
XLA Ops:
  1.3 0.7 %copy-done.11 = s32[1,4,128]{2,1,0:T(4,128)S(1)} copy-done((s32[1,4,128]{2,1,0:T(4,128)S(1)}, s32[1,4,128]{2,1,0:T(4,128)}, u32[]{:S(2)}) %copy-start.11) | copy-done | bytes 2072
  2.0 0.9 %copy-done.2 = bf16[512,128]{1,0:T(8,128)(2,1)S(1)} copy-done((bf16[512,128]{1,0:T(8,128)(2,1)S(1)}, bf16[512,128]{1,0:T(8,128)(2,1)}, u32[]{:S(2)}) %copy-start.2) | copy-done | bytes 131096
  2.9 9.5 %shard_map.256.halo_ref = bf16[512,128]{1,0:T(8,128)(2,1)S(1)} custom-call(bf16[512,128]{1,0:T(8,128)(2,1)S(1)} %copy-done.2, s32[4,128]{1,0:T(4,128)S(1)} %bitcast.13), custom_call_target="tpu_custom_call" | custom-call | tf_op jit(solution)/shard_map/pallas_call | solution.py:512
  12.5 0.0 copy-start
  12.5 1.0 %copy-done = bf16[1536,128]{1,0:T(8,128)(2,1)S(1)} copy-done((bf16[1536,128]{1,0:T(8,128)(2,1)S(1)}, bf16[1536,128]{1,0:T(8,128)(2,1)}, u32[]{:S(2)}) %copy-start) | copy-done | bytes 393240
  13.5 1.0 %copy-done.1 = bf16[1536,128]{1,0:T(8,128)(2,1)S(1)} copy-done((bf16[1536,128]{1,0:T(8,128)(2,1)S(1)}, bf16[1536,128]{1,0:T(8,128)(2,1)}, u32[]{:S(2)}) %copy-start.1) | copy-done | bytes 393240
  14.5 0.9 %copy-done.5 = bf16[384,128]{1,0:T(8,128)(2,1)S(1)} copy-done((bf16[384,128]{1,0:T(8,128)(2,1)S(1)}, bf16[384,128]{1,0:T(8,128)(2,1)}, u32[]{:S(2)}) %copy-start.5) | copy-done | bytes 98328
  15.4 0.8 %copy-done.6 = bf16[256,128]{1,0:T(8,128)(2,1)S(1)} copy-done((bf16[256,128]{1,0:T(8,128)(2,1)S(1)}, bf16[256,128]{1,0:T(8,128)(2,1)}, u32[]{:S(2)}) %copy-start.6) | copy-done | bytes 65560
  16.2 0.8 %copy-done.7 = bf16[128,128]{1,0:T(8,128)(2,1)S(1)} copy-done((bf16[128,128]{1,0:T(8,128)(2,1)S(1)}, bf16[128,128]{1,0:T(8,128)(2,1)}, u32[]{:S(2)}) %copy-start.7) | copy-done | bytes 32792
  17.0 0.8 %copy-done.8 = bf16[128,128]{1,0:T(8,128)(2,1)S(1)} copy-done((bf16[128,128]{1,0:T(8,128)(2,1)S(1)}, bf16[128,128]{1,0:T(8,128)(2,1)}, u32[]{:S(2)}) %copy-start.8) | copy-done | bytes 32792
  17.7 0.7 %copy-done.10 = s32[1536]{0:T(1024)S(1)} copy-done((s32[1536]{0:T(1024)S(1)}, s32[1536]{0:T(1024)}, u32[]{:S(2)}) %copy-start.10) | copy-done | bytes 6168
  18.4 39.8 %shard_map.257 = (bf16[512,128]{1,0:T(8,128)(2,1)S(1)}, bf16[512,128]{1,0:T(8,128)(2,1)S(1)}, bf16[512,128]{1,0:T(8,128)(2,1)S(1)}, bf16[1536,128]{1,0:T(8,128)(...) custom-call(bf16[512,128]{1,0:T(8,128)(2,1)S(1)} %copy-done.3, ...), custom_call_target="tpu_custom_call" | custom-call | tf_op jit(solution)/shard_map/pallas_call | solution.py:534
  58.3 0.7 %copy.42 = bf16[512,128]{1,0:T(8,128)(2,1)} copy(bf16[512,128]{1,0:T(8,128)(2,1)S(1)} %get-tuple-element.48) | data formatting | bytes 262144
  59.0 0.7 copy.43
  59.6 0.7 copy.44
  60.3 0.7 %copy.45 = bf16[1536,128]{1,0:T(8,128)(2,1)} copy(bf16[1536,128]{1,0:T(8,128)(2,1)S(1)} %get-tuple-element.51) | data formatting | bytes 786432
  61.0 0.7 %copy.46 = f32[384,128]{1,0:T(8,128)} copy(f32[384,128]{1,0:T(8,128)S(1)} %get-tuple-element.52) | data formatting | bytes 393216
  61.7 0.5 copy.47
  62.2 0.6 copy.48
  62.8 0.5 copy.49
  63.3 0.7 copy.50
  64.0 0.5 copy.51
  64.5 0.6 copy.52
  65.1 0.5 copy.53
  (22 shorter events, 0.0 us)
Async XLA Ops:
  1.3 11.1 %copy-start.9 = (s32[1536]{0:T(1024)S(1)}, s32[1536]{0:T(1024)}, u32[]{:S(2)}) copy-start(s32[1536]{0:T(1024)} %param.20) | copy-start | bytes 18436
  1.3 0.7 %copy-start.11 = (s32[1,4,128]{2,1,0:T(4,128)S(1)}, s32[1,4,128]{2,1,0:T(4,128)}, u32[]{:S(2)}) copy-start(s32[1,4,128]{2,1,0:T(4,128)} %param.23) | copy-start | bytes 6148
  2.0 0.9 %copy-start.2 = (bf16[512,128]{1,0:T(8,128)(2,1)S(1)}, bf16[512,128]{1,0:T(8,128)(2,1)}, u32[]{:S(2)}) copy-start(bf16[512,128]{1,0:T(8,128)(2,1)} %stale_ref.1) | copy-start | bytes 393220
  2.9 9.5 %copy-start.3 = (bf16[512,128]{1,0:T(8,128)(2,1)S(1)}, bf16[512,128]{1,0:T(8,128)(2,1)}, u32[]{:S(2)}) copy-start(bf16[512,128]{1,0:T(8,128)(2,1)} %lat_ref.1) | copy-start | bytes 393220
  2.9 9.6 %copy-start.4 = (bf16[512,128]{1,0:T(8,128)(2,1)S(1)}, bf16[512,128]{1,0:T(8,128)(2,1)}, u32[]{:S(2)}) copy-start(bf16[512,128]{1,0:T(8,128)(2,1)} %ncot_ref.1) | copy-start | bytes 393220
  2.9 9.6 %copy-start.12 = (f32[128]{0:T(128)S(1)}, f32[128]{0:T(128)}, u32[]{:S(2)}) copy-start(f32[128]{0:T(128)} %param.27) | copy-start | bytes 1540
  2.9 9.6 %copy-start.13 = (f32[128]{0:T(128)S(1)}, f32[128]{0:T(128)}, u32[]{:S(2)}) copy-start(f32[128]{0:T(128)} %param.29) | copy-start | bytes 1540
  2.9 9.6 %copy-start.14 = (f32[128]{0:T(128)S(1)}, f32[128]{0:T(128)}, u32[]{:S(2)}) copy-start(f32[128]{0:T(128)} %param.31) | copy-start | bytes 1540
  2.9 9.6 %copy-start.15 = (f32[128]{0:T(128)S(1)}, f32[128]{0:T(128)}, u32[]{:S(2)}) copy-start(f32[128]{0:T(128)} %param.33) | copy-start | bytes 1540
  12.5 1.0 %copy-start = (bf16[1536,128]{1,0:T(8,128)(2,1)S(1)}, bf16[1536,128]{1,0:T(8,128)(2,1)}, u32[]{:S(2)}) copy-start(bf16[1536,128]{1,0:T(8,128)(2,1)} %edge_ref.1) | copy-start | bytes 1179652
  13.5 1.0 %copy-start.1 = (bf16[1536,128]{1,0:T(8,128)(2,1)S(1)}, bf16[1536,128]{1,0:T(8,128)(2,1)}, u32[]{:S(2)}) copy-start(bf16[1536,128]{1,0:T(8,128)(2,1)} %ecot_ref.1) | copy-start | bytes 1179652
  14.5 0.9 %copy-start.5 = (bf16[384,128]{1,0:T(8,128)(2,1)S(1)}, bf16[384,128]{1,0:T(8,128)(2,1)}, u32[]{:S(2)}) copy-start(bf16[384,128]{1,0:T(8,128)(2,1)} %w1_ref.1) | copy-start | bytes 294916
  15.4 0.8 %copy-start.6 = (bf16[256,128]{1,0:T(8,128)(2,1)S(1)}, bf16[256,128]{1,0:T(8,128)(2,1)}, u32[]{:S(2)}) copy-start(bf16[256,128]{1,0:T(8,128)(2,1)} %nw1_ref.1) | copy-start | bytes 196612
  16.2 0.8 %copy-start.7 = (bf16[128,128]{1,0:T(8,128)(2,1)S(1)}, bf16[128,128]{1,0:T(8,128)(2,1)}, u32[]{:S(2)}) copy-start(bf16[128,128]{1,0:T(8,128)(2,1)} %w2_ref.1) | copy-start | bytes 98308
  17.0 0.8 %copy-start.8 = (bf16[128,128]{1,0:T(8,128)(2,1)S(1)}, bf16[128,128]{1,0:T(8,128)(2,1)}, u32[]{:S(2)}) copy-start(bf16[128,128]{1,0:T(8,128)(2,1)} %nw2_ref.1) | copy-start | bytes 98308
  17.7 0.7 %copy-start.10 = (s32[1536]{0:T(1024)S(1)}, s32[1536]{0:T(1024)}, u32[]{:S(2)}) copy-start(s32[1536]{0:T(1024)} %param.21) | copy-start | bytes 18436

commit v2 on v1

--- a/solution.py
+++ b/solution.py
@@ -15,7 +15,7 @@
 NODES = 512
 EDGES = 1536
 HALO = 128
-CHUNK = 256
+CHUNK = 768
 TILE = 32
 NEAR = 32
 FAR = 16
@@ -26,43 +26,44 @@
 ROW_EDGE_FIRST = 512
 ROW_SMALL = 896
 
-CORE = ("s", 1, 2)
-Y_HI = ("s", 2, 4)
-X = ("s", 8, 4)
-Y_LO = ("c", 1, 2)
-Z_0 = ("c", 2, 2)
-Z_HI = ("c", 4, 4)
+CORE = ("s", 1, 2, 0)
+Y_HI = ("s", 2, 4, 2)
+X = ("s", 8, 4, 1)
+Y_LO = ("c", 1, 2, 1)
+Z_0 = ("c", 2, 2, 1)
+Z_HI = ("c", 4, 4, 2)
 
 
 class Group:
     def __init__(self, digits, s, c):
         self.s, self.c = s, c
         self.pos = 0
-        self.peers = [(0, 0, 0, 0)]
+        peers = [(0, 0, 0, 0, 0)]
         size = 1
-        for axis, stride, n in digits:
+        for axis, stride, n, apart in digits:
             d = ((s if axis == "s" else c) // stride) % n
             self.pos = self.pos + d * size
             grown = []
             for k in range(n):
                 q = (d + k) % n if k else d
                 step = (q - d) * stride if k else 0
-                for key, ds, dc, at in self.peers:
+                for hops, key, ds, dc, at in peers:
                     grown.append(
                         (
+                            hops + min(k, n - k) * apart,
                             key + k * size,
                             ds + step if axis == "s" else ds,
                             dc + step if axis == "c" else dc,
                             at + q * size,
                         )
                     )
-            self.peers = grown
+            peers = grown
             size *= n
         self.size = size
-        self.peers = sorted(self.peers, key=lambda p: p[0])[1:]
+        self.peers = sorted((p for p in peers if p[1]), key=lambda p: (-p[0], p[1]))
 
     def others(self):
-        for key, ds, dc, at in self.peers:
+        for _, key, ds, dc, at in self.peers:
             yield key, (self.s + ds, self.c + dc), at
 
 
@@ -127,7 +128,54 @@
 BACK = (1, 0, 3, 2)
 
 
-def halo_kernel(stale_ref, list_ref, halo_ref, picked, landed, send_sem, recv_sem):
+def first_kernel(
+    stale_hbm,
+    list_hbm,
+    snd_hbm,
+    rcv_hbm,
+    lat_hbm,
+    edge_hbm,
+    w1_hbm,
+    b1_hbm,
+    w2_hbm,
+    g_hbm,
+    nw1_hbm,
+    nb1_hbm,
+    nw2_hbm,
+    ng_hbm,
+    ncot_hbm,
+    ecot_hbm,
+    count_smem,
+    list_ref,
+    snd_ref,
+    rcv_ref,
+    lat_ref,
+    edge_ref,
+    w1_ref,
+    b1_ref,
+    w2_ref,
+    g_ref,
+    nw1_ref,
+    nb1_ref,
+    nw2_ref,
+    ng_ref,
+    ncot_ref,
+    ecot_ref,
+    halo_ref,
+    count_ref,
+    hot_h_ref,
+    hot_r_ref,
+    hot_rt_ref,
+    rows_s_ref,
+    rows_r_ref,
+    part_ref,
+    stale_ref,
+    picked,
+    landed,
+    load_sem,
+    send_sem,
+    recv_sem,
+):
     s, c, to, count = place()
     barrier = pltpu.get_barrier_semaphore()
     for where, ok in to:
@@ -136,6 +184,29 @@
         def _(where=where):
             pl.semaphore_signal(barrier, inc=1, device_id=where, device_id_type=MESH)
 
+    pairs = [
+        (list_hbm, list_ref),
+        (stale_hbm, stale_ref),
+        (snd_hbm, snd_ref),
+        (rcv_hbm, rcv_ref),
+        (lat_hbm, lat_ref),
+        (edge_hbm, edge_ref),
+        (w1_hbm, w1_ref),
+        (b1_hbm, b1_ref),
+        (w2_hbm, w2_ref),
+        (g_hbm, g_ref),
+        (nw1_hbm, nw1_ref),
+        (nb1_hbm, nb1_ref),
+        (nw2_hbm, nw2_ref),
+        (ng_hbm, ng_ref),
+        (ncot_hbm, ncot_ref),
+        (ecot_hbm, ecot_ref),
+    ]
+    loads = [pltpu.make_async_copy(a, b, load_sem.at[k]) for k, (a, b) in enumerate(pairs)]
+    for load in loads:
+        load.start()
+    loads[0].wait()
+    loads[1].wait()
     table = jnp.concatenate([stale_ref[:256, :], stale_ref[256:, :]], axis=1)
     for k in range(4):
         col = columns_of(list_ref, k, 1)
@@ -160,6 +231,35 @@
         def _(k=k):
             copy(k).start()
 
+    for load in loads[2:]:
+        load.wait()
+    alive_count = count_smem[0]
+    count_ref[...] = jnp.full((8, W), alive_count, jnp.int32)
+    lat = lat_ref[...]
+    per = CHUNK // W
+    lane = lax.broadcasted_iota(jnp.int32, (1, W), 1)
+
+    def own_part(i, carry):
+        at = pl.ds(pl.multiple_of(i * CHUNK, CHUNK), CHUNK)
+        col_s = columns_of(snd_ref, i * per, per)
+        col_r = columns_of(rcv_ref, i * per, per)
+        row_at = lax.broadcasted_iota(jnp.int32, (CHUNK, W), 0) + i * CHUNK
+        hot = hot_rows(jnp.where(row_at < alive_count, col_r, -1), 4)
+        hot_r_ref[at, :] = hot
+        rows_r = dot(hot, lat).astype(BF16)
+        rows_r_ref[at, :] = rows_r
+        rows_s = dot(hot_rows(col_s, 4), lat).astype(BF16)
+        rows_s_ref[at, :] = rows_s
+        hot_h_ref[at, :] = hot_rows(col_s - NODES, 4)
+        joined = jnp.concatenate([edge_ref[at, :], rows_s, rows_r], axis=1)
+        part_ref[at, :] = dot(joined, w1_ref[...]) + b1_ref[...]
+        return carry
+
+    lax.fori_loop(0, EDGES // CHUNK, own_part, 0)
+    for k in range(EDGES // W):
+        row = jnp.where(lane + k * W < alive_count, rcv_ref[k : k + 1, :], -1)
+        hot_rt_ref[:, k * W : (k + 1) * W] = hot_cols(row, NODES)
+
     for k in range(4):
         has = to[BACK[k]][1]
 
@@ -180,15 +280,11 @@
 
 
 def layer_kernel(
-    lat_ref,
-    halo_ref,
-    edge_ref,
+    list_ref,
     snd_ref,
     rcv_ref,
-    count_ref,
-    list_ref,
-    ncot_ref,
-    ecot_ref,
+    lat_ref,
+    edge_ref,
     w1_ref,
     b1_ref,
     w2_ref,
@@ -197,32 +293,34 @@
     nb1_ref,
     nw2_ref,
     ng_ref,
+    ncot_ref,
+    ecot_ref,
+    halo_ref,
+    count_ref,
+    hot_h_ref,
+    hot_r_ref,
+    hot_rt_ref,
+    rows_s_ref,
+    rows_r_ref,
+    part_ref,
     new_ref,
     latg_ref,
     staleg_ref,
     edgeg_ref,
-    gw1_ref,
-    gb1_ref,
-    gw2_ref,
-    gg_ref,
-    gnw1_ref,
-    gnb1_ref,
-    gnw2_ref,
-    gng_ref,
-    hot_r,
-    rows_sr,
+    total,
+    rows_s,
     hidden,
     slope,
     xhat_s,
     rstd_s,
     values,
+    d_recv,
     d_pre,
     pack,
     near_in,
     near_sum,
     far_in,
     far_sum,
-    total,
     halo_out,
     halo_in,
     near_send,
@@ -238,43 +336,24 @@
     near = Group((CORE, X, Y_LO, Z_0), s, c)
     far = Group((Y_HI, Z_HI), s, c)
     barrier = pltpu.get_barrier_semaphore()
+    for group in (far, near):
+        for _, where, _ in group.others():
+            pl.semaphore_signal(barrier, inc=1, device_id=where, device_id_type=MESH)
     for where, ok in to:
 
         @pl.when(ok)
         def _(where=where):
             pl.semaphore_signal(barrier, inc=1, device_id=where, device_id_type=MESH)
 
-    for group in (far, near):
-        for _, where, _ in group.others():
-            pl.semaphore_signal(barrier, inc=1, device_id=where, device_id_type=MESH)
-
-    alive_count = count_ref[0]
     lat = lat_ref[...]
-    table_s = jnp.concatenate([lat, halo_ref[...]], axis=1)
-    table_r = jnp.concatenate([lat[:256, :], lat[256:, :]], axis=1)
     gain = g_ref[...]
     per = CHUNK // W
 
-    def alive_rows(i):
-        at = lax.broadcasted_iota(jnp.int32, (CHUNK, W), 0) + i * CHUNK
-        return at < alive_count
-
     def forward(i, carry):
         at = pl.ds(pl.multiple_of(i * CHUNK, CHUNK), CHUNK)
-        col_s = columns_of(snd_ref, i * per, per)
-        col_r = columns_of(rcv_ref, i * per, per)
-        alive = alive_rows(i)
-        both = dot(hot_rows(col_s & 511, 4), table_s)
-        rows_s = jnp.where(col_s < 512, both[:, :W], both[:, W:]).astype(BF16)
-        hot = hot_rows(jnp.where(alive, col_r & 255, -1), 2)
-        hot_r[at, :] = hot
-        both = dot(hot, table_r)
-        low = col_r < 256
-        rows_r = jnp.where(low, both[:, :W], both[:, W:]).astype(BF16)
-        edge = edge_ref[at, :]
-        joined = jnp.concatenate([edge, rows_s, rows_r], axis=1)
-        rows_sr[at, :] = joined
-        pre = dot(joined, w1_ref[...]) + b1_ref[...]
+        rows_h = dot(hot_h_ref[at, :], halo_ref[...]).astype(BF16)
+        rows_s[at, :] = rows_s_ref[at, :] + rows_h
+        pre = part_ref[at, :] + dot(rows_h, w1_ref[W : 2 * W, :])
         gate = sigmoid(pre)
         act = pre * gate
         slope[at, :] = gate + act * (1.0 - gate)
@@ -283,24 +362,11 @@
         xhat, rstd = normed(dot(act, w2_ref[...]))
         xhat_s[at, :] = xhat
         rstd_s[at, :] = jnp.broadcast_to(rstd, xhat.shape)
-        new = edge.astype(F32) + xhat * gain
-        values[at, :] = jnp.concatenate(
-            [jnp.where(low, new, 0.0).astype(BF16), jnp.where(low, 0.0, new).astype(BF16)], axis=1
-        )
+        values[at, :W] = (edge_ref[at, :].astype(F32) + xhat * gain).astype(BF16)
         return carry
 
     lax.fori_loop(0, EDGES // CHUNK, forward, 0)
-
-    def masked_receivers():
-        at = lax.broadcasted_iota(jnp.int32, (1, W), 1)
-        rows = []
-        for k in range(EDGES // W):
-            rows.append(jnp.where(at + k * W < alive_count, rcv_ref[k : k + 1, :] & 255, -1))
-        return jnp.concatenate(rows, axis=1)
-
-    hot_rt = hot_cols(masked_receivers(), 256)
-    agg = dot(hot_rt, values[...])
-    agg = jnp.concatenate([agg[:, :W], agg[:, W:]], axis=0).astype(BF16)
+    agg = dot(hot_rt_ref[...], values[:, :W]).astype(BF16)
 
     node_in = jnp.concatenate([lat, agg], axis=1)
     pre = dot(node_in, nw1_ref[...]) + nb1_ref[...]
@@ -322,15 +388,13 @@
     d_in = dot_nt(dp, nw1_ref[...])
     own = dy + d_in[:, :W]
     d_agg = d_in[:, W:].astype(BF16)
-    table_d = jnp.concatenate([d_agg[:256, :], d_agg[256:, :]], axis=1)
 
     def backward(i, carry):
         d_gain, d_bias = carry
         at = pl.ds(pl.multiple_of(i * CHUNK, CHUNK), CHUNK)
-        col_r = columns_of(rcv_ref, i * per, per)
-        both = dot(hot_r[at, :], table_d)
-        ct = ecot_ref[at, :].astype(F32) + jnp.where(col_r < 256, both[:, :W], both[:, W:])
-        dy = jnp.where(alive_rows(i), ct, 0.0)
+        ct = ecot_ref[at, :].astype(F32) + dot(hot_r_ref[at, :], d_agg)
+        row_at = lax.broadcasted_iota(jnp.int32, (CHUNK, W), 0) + i * CHUNK
+        dy = jnp.where(row_at < count_ref[0:1, :], ct, 0.0)
         xhat = xhat_s[at, :]
         d_gain = d_gain + jnp.sum(dy * xhat, axis=0, keepdims=True)
         dz = normed_back(dy * gain, xhat, rstd_s[at, :]).astype(BF16)
@@ -344,7 +408,9 @@
     zero = jnp.zeros((1, W), F32)
     d_gain, d_bias = lax.fori_loop(0, EDGES // CHUNK, backward, (zero, zero))
     pack[ROW_EDGE_SECOND : ROW_EDGE_SECOND + 128, :] = dot_tn(hidden[...], values[:, :W]).astype(BF16)
-    pack[ROW_EDGE_FIRST : ROW_EDGE_FIRST + 384, :] = dot_tn(rows_sr[...], d_pre[...]).astype(BF16)
+    for k, rows in enumerate((edge_ref, rows_s, rows_r_ref)):
+        first = ROW_EDGE_FIRST + W * k
+        pack[first : first + W, :] = dot_tn(rows[...], d_pre[...]).astype(BF16)
     pack[ROW_SMALL:, :] = jnp.concatenate(
         [d_bias, d_gain, d_nbias, d_ngain, jnp.zeros((PACK - ROW_SMALL - 4, W), F32)], axis=0
     ).astype(BF16)
@@ -369,11 +435,7 @@
         values[at, :] = jnp.concatenate(
             [jnp.where(mine, d_s, 0.0).astype(BF16), jnp.where(mine, 0.0, d_s).astype(BF16)], axis=1
         )
-        low = columns_of(rcv_ref, i * per, per) < 256
-        d_r = d_joined[:, 2 * W :]
-        rows_sr[at, : 2 * W] = jnp.concatenate(
-            [jnp.where(low, d_r, 0.0).astype(BF16), jnp.where(low, 0.0, d_r).astype(BF16)], axis=1
-        )
+        d_recv[at, :] = d_joined[:, 2 * W :].astype(BF16)
         return carry
 
     lax.fori_loop(0, EDGES // CHUNK, spread, 0)
@@ -398,10 +460,8 @@
         def _(k=k):
             back(k).start()
 
-    spread_r = dot(hot_cols(masked_receivers(), 256), rows_sr[:, : 2 * W])
-    latg_ref[...] = (
-        own + spread_s[:, :W] + jnp.concatenate([spread_r[:, :W], spread_r[:, W:]], axis=0)
-    ).astype(BF16)
+    spread_r = dot(hot_rt_ref[...], d_recv[...])
+    latg_ref[...] = (own + spread_s[:, :W] + spread_r).astype(BF16)
 
     mine = pl.ds(pl.multiple_of(near.pos * TILE, TILE), TILE)
     pltpu.make_async_copy(near_in, near_in, near_recv).wait()
@@ -462,29 +522,46 @@
     rest = total.at[pl.ds(0, PACK - TILE)]
     pltpu.make_async_copy(rest, rest, all_recv).wait()
     total[mine, :] = far_sum[...]
+
+    for k in range(4):
+
+        @pl.when(to[BACK[k]][1])
+        def _(k=k):
+            back(k).wait_send()
+
+    pltpu.make_async_copy(near_in, near_in, near_send).wait()
+    pltpu.make_async_copy(far_in.at[pl.ds(0, FAR - 1)], far_in.at[pl.ds(0, FAR - 1)], far_send).wait()
+    pltpu.make_async_copy(rest, rest, all_send).wait()
+
+
+def last_kernel(*refs):
+    bulk, total = refs[:4], refs[4]
+    outs = refs[5:17]
+    scaled, sem = refs[17:25], refs[25]
+    copies = [pltpu.make_async_copy(bulk[k], outs[k], sem.at[k]) for k in range(4)]
+    for copy in copies:
+        copy.start()
     sums = total[...].astype(F32)
     entries = ROW_SMALL * W + 4 * W
     squares = jnp.sum(sums * sums)
     factor = jnp.minimum(1.0, math.sqrt(entries) * lax.rsqrt(jnp.full((1, W), squares, F32)))
-    sums = sums * factor
-    gnw1_ref[...] = sums[ROW_NODE_FIRST : ROW_NODE_FIRST + 256, :]
-    gnw2_ref[...] = sums[ROW_NODE_SECOND : ROW_NODE_SECOND + 128, :]
-    gw2_ref[...] = sums[ROW_EDGE_SECOND : ROW_EDGE_SECOND + 128, :]
-    gw1_ref[...] = sums[ROW_EDGE_FIRST : ROW_EDGE_FIRST + 384, :]
-    gb1_ref[...] = sums[ROW_SMALL : ROW_SMALL + 1, :]
-    gg_ref[...] = sums[ROW_SMALL + 1 : ROW_SMALL + 2, :]
-    gnb1_ref[...] = sums[ROW_SMALL + 2 : ROW_SMALL + 3, :]
-    gng_ref[...] = sums[ROW_SMALL + 3 : ROW_SMALL + 4, :]
-
-    for k in range(4):
-
-        @pl.when(to[BACK[k]][1])
-        def _(k=k):
-            back(k).wait_send()
-
-    pltpu.make_async_copy(near_in, near_in, near_send).wait()
-    pltpu.make_async_copy(far_in.at[pl.ds(0, FAR - 1)], far_in.at[pl.ds(0, FAR - 1)], far_send).wait()
-    pltpu.make_async_copy(rest, rest, all_send).wait()
+    rows = (
+        (ROW_EDGE_FIRST, 384),
+        (ROW_SMALL, 1),
+        (ROW_EDGE_SECOND, 128),
+        (ROW_SMALL + 1, 1),
+        (ROW_NODE_FIRST, 256),
+        (ROW_SMALL + 2, 1),
+        (ROW_NODE_SECOND, 128),
+        (ROW_SMALL + 3, 1),
+    )
+    for k, (first, height) in enumerate(rows):
+        scaled[k][...] = sums[first : first + height, :] * factor
+        copy = pltpu.make_async_copy(scaled[k], outs[4 + k], sem.at[4 + k])
+        copy.start()
+        copies.append(copy)
+    for copy in copies:
+        copy.wait()
 
 
 def per_device(
@@ -507,81 +584,23 @@
     node_gain,
 ):
     vmem = pl.BlockSpec(memory_space=pltpu.VMEM)
-    smem = pl.BlockSpec(memory_space=pltpu.SMEM)
-    listed = send_list[0]
-    halo = pl.pallas_call(
-        halo_kernel,
-        out_shape=jax.ShapeDtypeStruct((4 * HALO, W), BF16),
-        in_specs=[vmem, vmem],
-        out_specs=vmem,
-        scratch_shapes=[
-            pltpu.VMEM((4, HALO, W), BF16),
-            pltpu.VMEM((4, HALO, W), BF16),
-            pltpu.SemaphoreType.DMA((4,)),
-            pltpu.SemaphoreType.DMA((4,)),
-        ],
-        compiler_params=pltpu.CompilerParams(
-            collective_id=0, has_side_effects=True, vmem_limit_bytes=16 * 2**20
-        ),
-    )(stale_latents, listed)
+    hbm = pl.BlockSpec(memory_space=pltpu.HBM)
 
     def row(v):
         return v.reshape(1, W)
 
-    def shape(rows, dtype):
-        return jax.ShapeDtypeStruct((rows, W), dtype)
-
-    outs = pl.pallas_call(
-        layer_kernel,
-        out_shape=(
-            shape(NODES, BF16),
-            shape(NODES, BF16),
-            shape(NODES, BF16),
-            shape(EDGES, BF16),
-            shape(384, F32),
-            shape(1, F32),
-            shape(128, F32),
-            shape(1, F32),
-            shape(256, F32),
-            shape(1, F32),
-            shape(128, F32),
-            shape(1, F32),
-        ),
-        in_specs=[vmem] * 5 + [smem] + [vmem] * 11,
-        out_specs=(vmem,) * 12,
-        scratch_shapes=[
-            pltpu.VMEM((EDGES, 256), BF16),
-            pltpu.VMEM((EDGES, 384), BF16),
-            pltpu.VMEM((EDGES, W), BF16),
-            pltpu.VMEM((EDGES, W), F32),
-            pltpu.VMEM((EDGES, W), F32),
-            pltpu.VMEM((EDGES, W), F32),
-            pltpu.VMEM((EDGES, 256), BF16),
-            pltpu.VMEM((EDGES, W), BF16),
-            pltpu.VMEM((PACK, W), BF16),
-            pltpu.VMEM((NEAR - 1, TILE, W), BF16),
-            pltpu.VMEM((TILE, W), BF16),
-            pltpu.VMEM((FAR, TILE, W), BF16),
-            pltpu.VMEM((TILE, W), BF16),
-            pltpu.VMEM((PACK, W), BF16),
-            pltpu.VMEM((4, HALO, W), BF16),
-            pltpu.VMEM((4, HALO, W), BF16),
-        ]
-        + [pltpu.SemaphoreType.DMA] * 6
-        + [pltpu.SemaphoreType.DMA((4,))] * 2,
-        compiler_params=pltpu.CompilerParams(
-            collective_id=1, has_side_effects=True, vmem_limit_bytes=48 * 2**20
-        ),
-    )(
-        latents,
-        halo,
-        edge_latents,
+    def far_away(v):
+        return pltpu.with_memory_space_constraint(v, pltpu.HBM)
+
+    def shape(rows, dtype, width=W):
+        return jax.ShapeDtypeStruct((rows, width), dtype)
+
+    fetched = (
+        send_list[0],
         senders.reshape(EDGES // W, W),
         receivers.reshape(EDGES // W, W),
-        edge_count,
-        listed,
-        node_cotangent,
-        edge_cotangent,
+        latents,
+        edge_latents,
         edge_first,
         row(edge_bias),
         edge_second,
@@ -590,7 +609,90 @@
         row(node_bias),
         node_second,
         row(node_gain),
+        node_cotangent,
+        edge_cotangent,
     )
+    made = (
+        shape(4 * HALO, BF16),
+        shape(8, jnp.int32),
+        shape(EDGES, BF16, 4 * HALO),
+        shape(EDGES, BF16, NODES),
+        shape(NODES, BF16, EDGES),
+        shape(EDGES, BF16),
+        shape(EDGES, BF16),
+        shape(EDGES, F32),
+    )
+    first = pl.pallas_call(
+        first_kernel,
+        out_shape=tuple(jax.ShapeDtypeStruct(v.shape, v.dtype) for v in fetched) + made,
+        in_specs=[hbm] * 16 + [pl.BlockSpec(memory_space=pltpu.SMEM)],
+        out_specs=(vmem,) * (len(fetched) + len(made)),
+        scratch_shapes=[
+            pltpu.VMEM((NODES, W), BF16),
+            pltpu.VMEM((4, HALO, W), BF16),
+            pltpu.VMEM((4, HALO, W), BF16),
+            pltpu.SemaphoreType.DMA((16,)),
+            pltpu.SemaphoreType.DMA((4,)),
+            pltpu.SemaphoreType.DMA((4,)),
+        ],
+        compiler_params=pltpu.CompilerParams(
+            collective_id=0, has_side_effects=True, vmem_limit_bytes=24 * 2**20
+        ),
+    )(*(far_away(v) for v in (stale_latents, *fetched)), edge_count)
+
+    second = pl.pallas_call(
+        layer_kernel,
+        out_shape=(
+            shape(NODES, BF16),
+            shape(NODES, BF16),
+            shape(NODES, BF16),
+            shape(EDGES, BF16),
+            shape(PACK, BF16),
+        ),
+        in_specs=[vmem] * len(first),
+        out_specs=(vmem,) * 5,
+        scratch_shapes=[
+            pltpu.VMEM((EDGES, W), BF16),
+            pltpu.VMEM((EDGES, W), BF16),
+            pltpu.VMEM((EDGES, W), F32),
+            pltpu.VMEM((EDGES, W), F32),
+            pltpu.VMEM((EDGES, W), F32),
+            pltpu.VMEM((EDGES, 256), BF16),
+            pltpu.VMEM((EDGES, W), BF16),
+            pltpu.VMEM((EDGES, W), BF16),
+            pltpu.VMEM((PACK, W), BF16),
+            pltpu.VMEM((NEAR - 1, TILE, W), BF16),
+            pltpu.VMEM((TILE, W), BF16),
+            pltpu.VMEM((FAR, TILE, W), BF16),
+            pltpu.VMEM((TILE, W), BF16),
+            pltpu.VMEM((4, HALO, W), BF16),
+            pltpu.VMEM((4, HALO, W), BF16),
+        ]
+        + [pltpu.SemaphoreType.DMA] * 6
+        + [pltpu.SemaphoreType.DMA((4,))] * 2,
+        compiler_params=pltpu.CompilerParams(
+            collective_id=1, has_side_effects=True, vmem_limit_bytes=32 * 2**20
+        ),
+    )(*first)
+
+    weights = (
+        shape(384, F32),
+        shape(1, F32),
+        shape(128, F32),
+        shape(1, F32),
+        shape(256, F32),
+        shape(1, F32),
+        shape(128, F32),
+        shape(1, F32),
+    )
+    outs = pl.pallas_call(
+        last_kernel,
+        out_shape=tuple(jax.ShapeDtypeStruct(v.shape, v.dtype) for v in second[:4]) + weights,
+        in_specs=[vmem] * 5,
+        out_specs=(hbm,) * 12,
+        scratch_shapes=[pltpu.VMEM(v.shape, F32) for v in weights] + [pltpu.SemaphoreType.DMA((12,))],
+        compiler_params=pltpu.CompilerParams(vmem_limit_bytes=16 * 2**20),
+    )(*second)
     return tuple(v.reshape(W) if v.shape[0] == 1 else v for v in outs)
 
 

time: 66.2 us -> 45.9 us (0.69)
  local copies, waits for them, and re-layouts: 14.9 us -> 0 us
  Pallas kernels: 49.3 us -> 44.4 us
    unnamed x44 -> x0, local copies, waits for them, and re-layouts: 14.9 us -> none
    pallas_call x1, Pallas kernels: 39.8 us -> 32.9 us  [per_device(): pl.pallas_call(layer_kernel, out_shape=(shape(NODES, BF16), shape(NODES,...]
    pallas_call x1 -> x2, Pallas kernels: 9.49 us -> 11.5 us  [the longest x1 10.3 us: per_device(): pl.pallas_call(first_kernel, out_shape=tuple((jax.ShapeDtypeStruct(v.shap...]
where the time goes in v2:
time: 45.9 us; the launch traced here: 45.7 us
  Pallas kernels  44.4 us (97%)
  between operations  1.31 us (3%)
    pallas_call x1, Pallas kernels, per_device(): pl.pallas_call(layer_kernel, out_shape=(shape(NODES, BF16), shape(NODES,...  32.9 us
    pallas_call x1, Pallas kernels, per_device(): pl.pallas_call(first_kernel, out_shape=tuple((jax.ShapeDtypeStruct(v.shap...  10.3 us
    pallas_call x1, Pallas kernels, per_device(): pl.pallas_call(last_kernel, out_shape=tuple((jax.ShapeDtypeStruct(v.shape...  1.26 us

profile of v2, /device:TPU:1, one launch (start us, length us, event | category | flops | bytes accessed | tf_op | source)
XLA Modules:
  0.0 45.7 jit_solution(10650162150441868169)
XLA Ops:
  1.3 10.3 %shard_map.256 = (s32[4,128]{1,0:T(4,128)S(1)}, s32[12,128]{1,0:T(8,128)S(1)}, s32[12,128]{1,0:T(8,128)S(1)}, bf16[512,128]{1,0:T(8,128)(2,1)S(1)}, bf16[1536,12...) custom-call(bf16[512,128]{1,0:T(8,128)(2,1)} %stale_hbm.1, ...), custom_call_target="tpu_custom_call" | custom-call | tf_op jit(solution)/shard_map/pallas_call | solution.py:625
  11.6 32.9 %shard_map.257 = (bf16[512,128]{1,0:T(8,128)(2,1)S(1)}, bf16[512,128]{1,0:T(8,128)(2,1)S(1)}, bf16[512,128]{1,0:T(8,128)(2,1)S(1)}, bf16[1536,128]{1,0:T(8,128)(2,1)S(1)}, bf16[1024,128]{1,0:T(8,128)(2,1)S(1)}) custom-call(s32[4,128]{1,0:T(4,128)S(1)} %get-tuple-element.52.list_ref, s32[12,128]{1,0:T(8,128)S(1)} %get-tuple-element.53.snd_ref, ...), custom_call_target="tpu_custom_call" | custom-call | tf_op jit(solution)/shard_map/pallas_call | solution.py:643
  44.5 1.3 %shard_map.258 = (bf16[512,128]{1,0:T(8,128)(2,1)}, bf16[512,128]{1,0:T(8,128)(2,1)}, bf16[512,128]{1,0:T(8,128)(2,1)}, bf16[1536,128]{1,0:T(8,128)(2,1)}, f32[3...) custom-call(bf16[512,128]{1,0:T(8,128)(2,1)S(1)} %get-tuple-element., ...), custom_call_target="tpu_custom_call" | custom-call | tf_op jit(solution)/shard_map/pallas_call | solution.py:688

commit v3 on v2

--- a/solution.py
+++ b/solution.py
@@ -16,10 +16,12 @@
 EDGES = 1536
 HALO = 128
 CHUNK = 768
-TILE = 32
+TILE = 16
 NEAR = 32
 FAR = 16
-PACK = TILE * NEAR
+HALF = TILE * NEAR
+OWNERS = (32, 25)
+PACK = TILE * sum(OWNERS)
 ROW_NODE_FIRST = 0
 ROW_NODE_SECOND = 256
 ROW_EDGE_SECOND = 384
@@ -408,23 +410,97 @@
     zero = jnp.zeros((1, W), F32)
     d_gain, d_bias = lax.fori_loop(0, EDGES // CHUNK, backward, (zero, zero))
     pack[ROW_EDGE_SECOND : ROW_EDGE_SECOND + 128, :] = dot_tn(hidden[...], values[:, :W]).astype(BF16)
+
+    def owner(half, at):
+        return at < OWNERS[half]
+
+    def tile(half, at):
+        return pl.ds(pl.multiple_of(half * HALF + at * TILE, TILE), TILE)
+
+    def await_tiles(sem, count):
+        tiles = pack.at[pl.ds(0, count * TILE)]
+        pltpu.make_async_copy(tiles, tiles, sem).wait()
+
+    def near_start(half):
+        for key, where, at in near.others():
+
+            @pl.when(owner(half, at))
+            def _(key=key, where=where, at=at):
+                pltpu.make_async_remote_copy(
+                    src_ref=pack.at[tile(half, at)],
+                    dst_ref=near_in.at[half, key - 1],
+                    send_sem=near_send.at[half],
+                    recv_sem=near_recv.at[half],
+                    device_id=where,
+                    device_id_type=MESH,
+                ).start()
+
+    def far_start(half):
+        @pl.when(owner(half, near.pos))
+        def _():
+            await_tiles(near_recv.at[half], NEAR - 1)
+            acc = pack[tile(half, near.pos), :].astype(F32)
+            for k in range(NEAR - 1):
+                acc = acc + near_in[half, k].astype(F32)
+            near_sum[half] = acc.astype(BF16)
+            for key, where, at in far.others():
+                pltpu.make_async_remote_copy(
+                    src_ref=near_sum.at[half],
+                    dst_ref=far_in.at[half, far.pos],
+                    send_sem=far_send.at[half],
+                    recv_sem=far_recv.at[half],
+                    device_id=where,
+                    device_id_type=MESH,
+                ).start()
+
+    def all_start(half):
+        @pl.when(owner(half, near.pos))
+        def _():
+            await_tiles(far_recv.at[half], FAR - 1)
+            far_in[half, far.pos] = near_sum[half]
+            acc = far_in[half, 0].astype(F32)
+            for k in range(1, FAR):
+                acc = acc + far_in[half, k].astype(F32)
+            far_sum[half] = acc.astype(BF16)
+            for key, where, at in near.others():
+                pltpu.make_async_remote_copy(
+                    src_ref=far_sum.at[half],
+                    dst_ref=total.at[tile(half, near.pos)],
+                    send_sem=all_send.at[half],
+                    recv_sem=all_recv.at[half],
+                    device_id=where,
+                    device_id_type=MESH,
+                ).start()
+            total[tile(half, near.pos), :] = far_sum[half]
+
+    def await_owners(sem, half):
+        @pl.when(owner(half, near.pos))
+        def _():
+            await_tiles(sem, OWNERS[half] - 1)
+
+        if OWNERS[half] < NEAR:
+
+            @pl.when(jnp.logical_not(owner(half, near.pos)))
+            def _():
+                await_tiles(sem, OWNERS[half])
+
+    def finish(half):
+        await_owners(near_send.at[half], half)
+
+        @pl.when(owner(half, near.pos))
+        def _():
+            await_tiles(far_send.at[half], FAR - 1)
+            await_tiles(all_send.at[half], NEAR - 1)
+
+    pl.semaphore_wait(barrier, count + (NEAR - 1) + (FAR - 1))
+    near_start(0)
     for k, rows in enumerate((edge_ref, rows_s, rows_r_ref)):
         first = ROW_EDGE_FIRST + W * k
         pack[first : first + W, :] = dot_tn(rows[...], d_pre[...]).astype(BF16)
     pack[ROW_SMALL:, :] = jnp.concatenate(
         [d_bias, d_gain, d_nbias, d_ngain, jnp.zeros((PACK - ROW_SMALL - 4, W), F32)], axis=0
     ).astype(BF16)
-
-    pl.semaphore_wait(barrier, count + (NEAR - 1) + (FAR - 1))
-    for key, where, at in near.others():
-        pltpu.make_async_remote_copy(
-            src_ref=pack.at[pl.ds(pl.multiple_of(at * TILE, TILE), TILE)],
-            dst_ref=near_in.at[key - 1],
-            send_sem=near_send,
-            recv_sem=near_recv,
-            device_id=where,
-            device_id_type=MESH,
-        ).start()
+    near_start(1)
 
     def spread(i, carry):
         at = pl.ds(pl.multiple_of(i * CHUNK, CHUNK), CHUNK)
@@ -463,21 +539,8 @@
     spread_r = dot(hot_rt_ref[...], d_recv[...])
     latg_ref[...] = (own + spread_s[:, :W] + spread_r).astype(BF16)
 
-    mine = pl.ds(pl.multiple_of(near.pos * TILE, TILE), TILE)
-    pltpu.make_async_copy(near_in, near_in, near_recv).wait()
-    acc = pack[mine, :].astype(F32)
-    for k in range(NEAR - 1):
-        acc = acc + near_in[k].astype(F32)
-    near_sum[...] = acc.astype(BF16)
-    for key, where, at in far.others():
-        pltpu.make_async_remote_copy(
-            src_ref=near_sum,
-            dst_ref=far_in.at[far.pos],
-            send_sem=far_send,
-            recv_sem=far_recv,
-            device_id=where,
-            device_id_type=MESH,
-        ).start()
+    far_start(0)
+    far_start(1)
 
     for k in range(4):
         has = to[k][1]
@@ -504,34 +567,18 @@
     stale = dot(hot_cols(listed, 256), jnp.concatenate(parts, axis=0))
     staleg_ref[...] = jnp.concatenate([stale[:, :W], stale[:, W:]], axis=0).astype(BF16)
 
-    pltpu.make_async_copy(far_in.at[pl.ds(0, FAR - 1)], far_in.at[pl.ds(0, FAR - 1)], far_recv).wait()
-    far_in[far.pos] = near_sum[...]
-    acc = far_in[0].astype(F32)
-    for k in range(1, FAR):
-        acc = acc + far_in[k].astype(F32)
-    far_sum[...] = acc.astype(BF16)
-    for key, where, at in near.others():
-        pltpu.make_async_remote_copy(
-            src_ref=far_sum,
-            dst_ref=total.at[mine],
-            send_sem=all_send,
-            recv_sem=all_recv,
-            device_id=where,
-            device_id_type=MESH,
-        ).start()
-    rest = total.at[pl.ds(0, PACK - TILE)]
-    pltpu.make_async_copy(rest, rest, all_recv).wait()
-    total[mine, :] = far_sum[...]
-
+    all_start(0)
+    all_start(1)
     for k in range(4):
 
         @pl.when(to[BACK[k]][1])
         def _(k=k):
             back(k).wait_send()
 
-    pltpu.make_async_copy(near_in, near_in, near_send).wait()
-    pltpu.make_async_copy(far_in.at[pl.ds(0, FAR - 1)], far_in.at[pl.ds(0, FAR - 1)], far_send).wait()
-    pltpu.make_async_copy(rest, rest, all_send).wait()
+    await_owners(all_recv.at[0], 0)
+    await_owners(all_recv.at[1], 1)
+    finish(0)
+    finish(1)
 
 
 def last_kernel(*refs):
@@ -661,14 +708,14 @@
             pltpu.VMEM((EDGES, W), BF16),
             pltpu.VMEM((EDGES, W), BF16),
             pltpu.VMEM((PACK, W), BF16),
-            pltpu.VMEM((NEAR - 1, TILE, W), BF16),
-            pltpu.VMEM((TILE, W), BF16),
-            pltpu.VMEM((FAR, TILE, W), BF16),
-            pltpu.VMEM((TILE, W), BF16),
+            pltpu.VMEM((2, NEAR - 1, TILE, W), BF16),
+            pltpu.VMEM((2, TILE, W), BF16),
+            pltpu.VMEM((2, FAR, TILE, W), BF16),
+            pltpu.VMEM((2, TILE, W), BF16),
             pltpu.VMEM((4, HALO, W), BF16),
             pltpu.VMEM((4, HALO, W), BF16),
         ]
-        + [pltpu.SemaphoreType.DMA] * 6
+        + [pltpu.SemaphoreType.DMA((2,))] * 6
         + [pltpu.SemaphoreType.DMA((4,))] * 2,
         compiler_params=pltpu.CompilerParams(
             collective_id=1, has_side_effects=True, vmem_limit_bytes=32 * 2**20

time: 45.9 us -> 44.3 us (0.965)
  Pallas kernels: 44.4 us -> 42.8 us
    pallas_call x1, Pallas kernels: 32.9 us -> 31.4 us  [per_device(): pl.pallas_call(layer_kernel, out_shape=(shape(NODES, BF16), shape(NODES,...]
where the time goes in v3:
time: 44.3 us; the launch traced here: 44.1 us
  Pallas kernels  42.8 us (97%)
  between operations  1.31 us (3%)
    pallas_call x1, Pallas kernels, per_device(): pl.pallas_call(layer_kernel, out_shape=(shape(NODES, BF16), shape(NODES,...  31.4 us
    pallas_call x1, Pallas kernels, per_device(): pl.pallas_call(first_kernel, out_shape=tuple((jax.ShapeDtypeStruct(v.shap...  10.3 us
    pallas_call x1, Pallas kernels, per_device(): pl.pallas_call(last_kernel, out_shape=tuple((jax.ShapeDtypeStruct(v.shape...  1.14 us

profile of v3, /device:TPU:1, one launch (start us, length us, event | category | flops | bytes accessed | tf_op | source)
XLA Modules:
  0.0 44.1 jit_solution(276905062168442187)
XLA Ops:
  1.3 10.3 %shard_map.256 = (s32[4,128]{1,0:T(4,128)S(1)}, s32[12,128]{1,0:T(8,128)S(1)}, s32[12,128]{1,0:T(8,128)S(1)}, bf16[512,128]{1,0:T(8,128)(2,1)S(1)}, bf16[1536,12...) custom-call(bf16[512,128]{1,0:T(8,128)(2,1)} %stale_hbm.1, ...), custom_call_target="tpu_custom_call" | custom-call | tf_op jit(solution)/shard_map/pallas_call | solution.py:672
  11.6 31.4 %shard_map.257 = (bf16[512,128]{1,0:T(8,128)(2,1)S(1)}, bf16[512,128]{1,0:T(8,128)(2,1)S(1)}, bf16[512,128]{1,0:T(8,128)(2,1)S(1)}, bf16[1536,128]{1,0:T(8,128)(2,1)S(1)}, bf16[912,128]{1,0:T(8,128)(2,1)S(1)}) custom-call(s32[4,128]{1,0:T(4,128)S(1)} %get-tuple-element.52.list_ref, s32[12,128]{1,0:T(8,128)S(1)} %get-tuple-element.53.snd_ref, ...), custom_call_target="tpu_custom_call" | custom-call | tf_op jit(solution)/shard_map/pallas_call | solution.py:690
  43.0 1.1 %shard_map.258 = (bf16[512,128]{1,0:T(8,128)(2,1)}, bf16[512,128]{1,0:T(8,128)(2,1)}, bf16[512,128]{1,0:T(8,128)(2,1)}, bf16[1536,128]{1,0:T(8,128)(2,1)}, f32[3...) custom-call(bf16[512,128]{1,0:T(8,128)(2,1)S(1)} %get-tuple-element., ...), custom_call_target="tpu_custom_call" | custom-call | tf_op jit(solution)/shard_map/pallas_call | solution.py:735

commit v4 on v3

--- a/solution.py
+++ b/solution.py
@@ -15,7 +15,7 @@
 NODES = 512
 EDGES = 1536
 HALO = 128
-CHUNK = 768
+CHUNK = 1536
 TILE = 16
 NEAR = 32
 FAR = 16
@@ -28,45 +28,53 @@
 ROW_EDGE_FIRST = 512
 ROW_SMALL = 896
 
-CORE = ("s", 1, 2, 0)
-Y_HI = ("s", 2, 4, 2)
-X = ("s", 8, 4, 1)
-Y_LO = ("c", 1, 2, 1)
-Z_0 = ("c", 2, 2, 1)
-Z_HI = ("c", 4, 4, 2)
-
-
-class Group:
-    def __init__(self, digits, s, c):
-        self.s, self.c = s, c
-        self.pos = 0
-        peers = [(0, 0, 0, 0, 0)]
-        size = 1
-        for axis, stride, n, apart in digits:
-            d = ((s if axis == "s" else c) // stride) % n
-            self.pos = self.pos + d * size
-            grown = []
-            for k in range(n):
-                q = (d + k) % n if k else d
-                step = (q - d) * stride if k else 0
-                for hops, key, ds, dc, at in peers:
-                    grown.append(
-                        (
-                            hops + min(k, n - k) * apart,
-                            key + k * size,
-                            ds + step if axis == "s" else ds,
-                            dc + step if axis == "c" else dc,
-                            at + q * size,
-                        )
-                    )
-            peers = grown
-            size *= n
-        self.size = size
-        self.peers = sorted((p for p in peers if p[1]), key=lambda p: (-p[0], p[1]))
-
-    def others(self):
-        for _, key, ds, dc, at in self.peers:
-            yield key, (self.s + ds, self.c + dc), at
+
+def ring_pair(p):
+    pair = ((p + 1) // 2) % 4
+    turned = ((pair + 1) // 2 + 1) % 2
+    return pair, ((p + 1) % 2 + turned) % 2
+
+
+def ring_place(pair, label):
+    turned = ((pair + 1) // 2 + 1) % 2
+    return (2 * pair + (label + turned) % 2 + 7) % 8
+
+
+class Peers:
+    def __init__(self, s, c):
+        core, x = s % 2, s // 8
+        y, z = ((s // 2) % 4) * 2 + c % 2, c // 2
+        (wy, ly), (wz, lz) = ring_pair(y), ring_pair(z)
+        cores = [core, 1 - core]
+        xs = [(x + k) % 4 for k in range(4)]
+        self.near_pos = core + 2 * x + 8 * ly + 16 * lz
+        self.far_pos = wy + 4 * wz
+        ys = [(y, ly), (ring_place(wy, 1 - ly), 1 - ly)]
+        zs = [(z, lz), (ring_place(wz, 1 - lz), 1 - lz)]
+        near = []
+        for kc in range(2):
+            for kx in range(4):
+                for ky in range(2):
+                    for kz in range(2):
+                        key = kc + 2 * kx + 8 * ky + 16 * kz
+                        hops = (0, 1, 2, 1)[kx] + ky + kz
+                        (py, qy), (pz, qz) = ys[ky], zs[kz]
+                        at = cores[kc] + 2 * xs[kx] + 8 * qy + 16 * qz
+                        near.append((-hops, key, self.device(xs[kx], py, pz, cores[kc]), at))
+        far = []
+        for ky in range(4):
+            for kz in range(4):
+                key = ky + 4 * kz
+                hops = (0, 2, 3, 2)[ky] + (0, 2, 3, 2)[kz]
+                py = ring_place((wy + ky) % 4, ly) if ky else y
+                pz = ring_place((wz + kz) % 4, lz) if kz else z
+                far.append((-hops, key, self.device(x, py, pz, core)))
+        self.near = [p[1:] for p in sorted(near, key=lambda p: p[:2]) if p[1]]
+        self.far = [p[1:] for p in sorted(far, key=lambda p: p[:2]) if p[1]]
+
+    @staticmethod
+    def device(x, y, z, core):
+        return 8 * x + 2 * (y // 2) + core, 2 * z + y % 2
 
 
 def dot(a, b):
@@ -335,12 +343,10 @@
     halo_recv,
 ):
     s, c, to, count = place()
-    near = Group((CORE, X, Y_LO, Z_0), s, c)
-    far = Group((Y_HI, Z_HI), s, c)
+    peers = Peers(s, c)
     barrier = pltpu.get_barrier_semaphore()
-    for group in (far, near):
-        for _, where, _ in group.others():
-            pl.semaphore_signal(barrier, inc=1, device_id=where, device_id_type=MESH)
+    for peer in peers.far + peers.near:
+        pl.semaphore_signal(barrier, inc=1, device_id=peer[1], device_id_type=MESH)
     for where, ok in to:
 
         @pl.when(ok)
@@ -422,7 +428,7 @@
         pltpu.make_async_copy(tiles, tiles, sem).wait()
 
     def near_start(half):
-        for key, where, at in near.others():
+        for key, where, at in peers.near:
 
             @pl.when(owner(half, at))
             def _(key=key, where=where, at=at):
@@ -436,17 +442,17 @@
                 ).start()
 
     def far_start(half):
-        @pl.when(owner(half, near.pos))
+        @pl.when(owner(half, peers.near_pos))
         def _():
             await_tiles(near_recv.at[half], NEAR - 1)
-            acc = pack[tile(half, near.pos), :].astype(F32)
+            acc = pack[tile(half, peers.near_pos), :].astype(F32)
             for k in range(NEAR - 1):
                 acc = acc + near_in[half, k].astype(F32)
             near_sum[half] = acc.astype(BF16)
-            for key, where, at in far.others():
+            for key, where in peers.far:
                 pltpu.make_async_remote_copy(
                     src_ref=near_sum.at[half],
-                    dst_ref=far_in.at[half, far.pos],
+                    dst_ref=far_in.at[half, peers.far_pos],
                     send_sem=far_send.at[half],
                     recv_sem=far_recv.at[half],
                     device_id=where,
@@ -454,40 +460,40 @@
                 ).start()
 
     def all_start(half):
-        @pl.when(owner(half, near.pos))
+        @pl.when(owner(half, peers.near_pos))
         def _():
             await_tiles(far_recv.at[half], FAR - 1)
-            far_in[half, far.pos] = near_sum[half]
+            far_in[half, peers.far_pos] = near_sum[half]
             acc = far_in[half, 0].astype(F32)
             for k in range(1, FAR):
                 acc = acc + far_in[half, k].astype(F32)
             far_sum[half] = acc.astype(BF16)
-            for key, where, at in near.others():
+            for key, where, at in peers.near:
                 pltpu.make_async_remote_copy(
                     src_ref=far_sum.at[half],
-                    dst_ref=total.at[tile(half, near.pos)],
+                    dst_ref=total.at[tile(half, peers.near_pos)],
                     send_sem=all_send.at[half],
                     recv_sem=all_recv.at[half],
                     device_id=where,
                     device_id_type=MESH,
                 ).start()
-            total[tile(half, near.pos), :] = far_sum[half]
+            total[tile(half, peers.near_pos), :] = far_sum[half]
 
     def await_owners(sem, half):
-        @pl.when(owner(half, near.pos))
+        @pl.when(owner(half, peers.near_pos))
         def _():
             await_tiles(sem, OWNERS[half] - 1)
 
         if OWNERS[half] < NEAR:
 
-            @pl.when(jnp.logical_not(owner(half, near.pos)))
+            @pl.when(jnp.logical_not(owner(half, peers.near_pos)))
             def _():
                 await_tiles(sem, OWNERS[half])
 
     def finish(half):
         await_owners(near_send.at[half], half)
 
-        @pl.when(owner(half, near.pos))
+        @pl.when(owner(half, peers.near_pos))
         def _():
             await_tiles(far_send.at[half], FAR - 1)
             await_tiles(all_send.at[half], NEAR - 1)

time: 44.3 us -> 43.6 us (0.984)
  Pallas kernels: 42.8 us -> 42.1 us
where the time goes in v4:
time: 43.6 us; the launch traced here: 43.4 us
  Pallas kernels  42.1 us (97%)
  between operations  1.31 us (3%)
    pallas_call x1, Pallas kernels, per_device(): pl.pallas_call(layer_kernel, out_shape=(shape(NODES, BF16), shape(NODES,...  31 us
    pallas_call x1, Pallas kernels, per_device(): pl.pallas_call(first_kernel, out_shape=tuple((jax.ShapeDtypeStruct(v.shap...  9.91 us
    pallas_call x1, Pallas kernels, per_device(): pl.pallas_call(last_kernel, out_shape=tuple((jax.ShapeDtypeStruct(v.shape...  1.14 us

profile of v4, /device:TPU:1, one launch (start us, length us, event | category | flops | bytes accessed | tf_op | source)
XLA Modules:
  0.0 43.4 jit_solution(10366689121757586884)
XLA Ops:
  1.3 9.9 %shard_map.256 = (s32[4,128]{1,0:T(4,128)S(1)}, s32[12,128]{1,0:T(8,128)S(1)}, s32[12,128]{1,0:T(8,128)S(1)}, bf16[512,128]{1,0:T(8,128)(2,1)S(1)}, bf16[1536,12...) custom-call(bf16[512,128]{1,0:T(8,128)(2,1)} %stale_hbm.1, ...), custom_call_target="tpu_custom_call" | custom-call | tf_op jit(solution)/shard_map/pallas_call | solution.py:678
  11.2 31.0 %shard_map.257 = (bf16[512,128]{1,0:T(8,128)(2,1)S(1)}, bf16[512,128]{1,0:T(8,128)(2,1)S(1)}, bf16[512,128]{1,0:T(8,128)(2,1)S(1)}, bf16[1536,128]{1,0:T(8,128)(2,1)S(1)}, bf16[912,128]{1,0:T(8,128)(2,1)S(1)}) custom-call(s32[4,128]{1,0:T(4,128)S(1)} %get-tuple-element.52.list_ref, s32[12,128]{1,0:T(8,128)S(1)} %get-tuple-element.53.snd_ref, ...), custom_call_target="tpu_custom_call" | custom-call | tf_op jit(solution)/shard_map/pallas_call | solution.py:696
  42.3 1.1 %shard_map.258 = (bf16[512,128]{1,0:T(8,128)(2,1)}, bf16[512,128]{1,0:T(8,128)(2,1)}, bf16[512,128]{1,0:T(8,128)(2,1)}, bf16[1536,128]{1,0:T(8,128)(2,1)}, f32[3...) custom-call(bf16[512,128]{1,0:T(8,128)(2,1)S(1)} %get-tuple-element., ...), custom_call_target="tpu_custom_call" | custom-call | tf_op jit(solution)/shard_map/pallas_call | solution.py:741

commit v5 on v4

--- a/solution.py
+++ b/solution.py
@@ -250,7 +250,7 @@
     lane = lax.broadcasted_iota(jnp.int32, (1, W), 1)
 
     def own_part(i, carry):
-        at = pl.ds(pl.multiple_of(i * CHUNK, CHUNK), CHUNK)
+        at = pl.ds(i * CHUNK, CHUNK)
         col_s = columns_of(snd_ref, i * per, per)
         col_r = columns_of(rcv_ref, i * per, per)
         row_at = lax.broadcasted_iota(jnp.int32, (CHUNK, W), 0) + i * CHUNK
@@ -265,7 +265,7 @@
         part_ref[at, :] = dot(joined, w1_ref[...]) + b1_ref[...]
         return carry
 
-    lax.fori_loop(0, EDGES // CHUNK, own_part, 0)
+    own_part(0, 0)
     for k in range(EDGES // W):
         row = jnp.where(lane + k * W < alive_count, rcv_ref[k : k + 1, :], -1)
         hot_rt_ref[:, k * W : (k + 1) * W] = hot_cols(row, NODES)
@@ -345,7 +345,7 @@
     s, c, to, count = place()
     peers = Peers(s, c)
     barrier = pltpu.get_barrier_semaphore()
-    for peer in peers.far + peers.near:
+    for peer in peers.near + peers.far:
         pl.semaphore_signal(barrier, inc=1, device_id=peer[1], device_id_type=MESH)
     for where, ok in to:
 
@@ -358,7 +358,7 @@
     per = CHUNK // W
 
     def forward(i, carry):
-        at = pl.ds(pl.multiple_of(i * CHUNK, CHUNK), CHUNK)
+        at = pl.ds(i * CHUNK, CHUNK)
         rows_h = dot(hot_h_ref[at, :], halo_ref[...]).astype(BF16)
         rows_s[at, :] = rows_s_ref[at, :] + rows_h
         pre = part_ref[at, :] + dot(rows_h, w1_ref[W : 2 * W, :])
@@ -373,7 +373,7 @@
         values[at, :W] = (edge_ref[at, :].astype(F32) + xhat * gain).astype(BF16)
         return carry
 
-    lax.fori_loop(0, EDGES // CHUNK, forward, 0)
+    forward(0, 0)
     agg = dot(hot_rt_ref[...], values[:, :W]).astype(BF16)
 
     node_in = jnp.concatenate([lat, agg], axis=1)
@@ -399,7 +399,7 @@
 
     def backward(i, carry):
         d_gain, d_bias = carry
-        at = pl.ds(pl.multiple_of(i * CHUNK, CHUNK), CHUNK)
+        at = pl.ds(i * CHUNK, CHUNK)
         ct = ecot_ref[at, :].astype(F32) + dot(hot_r_ref[at, :], d_agg)
         row_at = lax.broadcasted_iota(jnp.int32, (CHUNK, W), 0) + i * CHUNK
         dy = jnp.where(row_at < count_ref[0:1, :], ct, 0.0)
@@ -414,7 +414,7 @@
         return d_gain, d_bias
 
     zero = jnp.zeros((1, W), F32)
-    d_gain, d_bias = lax.fori_loop(0, EDGES // CHUNK, backward, (zero, zero))
+    d_gain, d_bias = backward(0, (zero, zero))
     pack[ROW_EDGE_SECOND : ROW_EDGE_SECOND + 128, :] = dot_tn(hidden[...], values[:, :W]).astype(BF16)
 
     def owner(half, at):
@@ -509,7 +509,7 @@
     near_start(1)
 
     def spread(i, carry):
-        at = pl.ds(pl.multiple_of(i * CHUNK, CHUNK), CHUNK)
+        at = pl.ds(i * CHUNK, CHUNK)
         d_joined = dot_nt(d_pre[at, :], w1_ref[...])
         edgeg_ref[at, :] = (xhat_s[at, :] + d_joined[:, :W]).astype(BF16)
         mine = columns_of(snd_ref, i * per, per) < 512
@@ -520,7 +520,7 @@
         d_recv[at, :] = d_joined[:, 2 * W :].astype(BF16)
         return carry
 
-    lax.fori_loop(0, EDGES // CHUNK, spread, 0)
+    spread(0, 0)
     senders = jnp.concatenate([snd_ref[k : k + 1, :] & 511 for k in range(EDGES // W)], axis=1)
     spread_s = dot(hot_cols(senders, 512), values[...])
     for k in range(4):

time: 43.6 us -> 44 us (level)
  no operation moved by 1% of the time
where the time goes in v5:
time: 44 us; the launch traced here: 43.8 us
  Pallas kernels  42.5 us (97%)
  between operations  1.31 us (3%)
    pallas_call x1, Pallas kernels, per_device(): pl.pallas_call(layer_kernel, out_shape=(shape(NODES, BF16), shape(NODES,...  31.4 us
    pallas_call x1, Pallas kernels, per_device(): pl.pallas_call(first_kernel, out_shape=tuple((jax.ShapeDtypeStruct(v.shap...  9.91 us
    pallas_call x1, Pallas kernels, per_device(): pl.pallas_call(last_kernel, out_shape=tuple((jax.ShapeDtypeStruct(v.shape...  1.14 us

profile of v5, /device:TPU:1, one launch (start us, length us, event | category | flops | bytes accessed | tf_op | source)
XLA Modules:
  0.0 43.8 jit_solution(12841118495433882870)
XLA Ops:
  1.3 9.9 %shard_map.256 = (s32[4,128]{1,0:T(4,128)S(1)}, s32[12,128]{1,0:T(8,128)S(1)}, s32[12,128]{1,0:T(8,128)S(1)}, bf16[512,128]{1,0:T(8,128)(2,1)S(1)}, bf16[1536,12...) custom-call(bf16[512,128]{1,0:T(8,128)(2,1)} %stale_hbm.1, ...), custom_call_target="tpu_custom_call" | custom-call | tf_op jit(solution)/shard_map/pallas_call | solution.py:678
  11.2 31.4 %shard_map.257 = (bf16[512,128]{1,0:T(8,128)(2,1)S(1)}, bf16[512,128]{1,0:T(8,128)(2,1)S(1)}, bf16[512,128]{1,0:T(8,128)(2,1)S(1)}, bf16[1536,128]{1,0:T(8,128)(2,1)S(1)}, bf16[912,128]{1,0:T(8,128)(2,1)S(1)}) custom-call(s32[4,128]{1,0:T(4,128)S(1)} %get-tuple-element.52.list_ref, s32[12,128]{1,0:T(8,128)S(1)} %get-tuple-element.53.snd_ref, ...), custom_call_target="tpu_custom_call" | custom-call | tf_op jit(solution)/shard_map/pallas_call | solution.py:696
  42.7 1.1 %shard_map.258 = (bf16[512,128]{1,0:T(8,128)(2,1)}, bf16[512,128]{1,0:T(8,128)(2,1)}, bf16[512,128]{1,0:T(8,128)(2,1)}, bf16[1536,128]{1,0:T(8,128)(2,1)}, f32[3...) custom-call(bf16[512,128]{1,0:T(8,128)(2,1)S(1)} %get-tuple-element., ...), custom_call_target="tpu_custom_call" | custom-call | tf_op jit(solution)/shard_map/pallas_call | solution.py:741
